TPU v7x, 128 devices: a whole 4x4x4 slice. The times are simulated.
128 devices in a mesh: dp: 16 (over z_lo, y, core), inner: 8 (over x, z_hi).
Axes of the slice: x: 4, y: 4, z: 4 (z_hi: 2, z_lo: 2; z = z_hi * 2 + z_lo), core: 2. Of those that a mesh axis runs over, the one named last changes fastest.
Arguments:
- image_embed: bfloat16 [16384, 1152], P(('dp', 'inner')), may hold values from -6 to 6
- text_embed: bfloat16 [16384, 1152], P(('dp', 'inner')), may hold values from -6 to 6
- image_head: bfloat16 [1152, 1152], replicated, may hold values from -0.1875 to 0.1875
- text_head: bfloat16 [1152, 1152], replicated, may hold values from -0.1875 to 0.1875
- pair_ids: int32 [16384], P(('dp', 'inner')), may hold values from 0 to 4095, never falling along the last dimension, each value on 1 to 8 neighbouring positions
- logit_scale: float32 [1], replicated, may hold values from 8 to 24
- logit_bias: float32 [1], replicated, may hold values from -4 to -1.5
Outputs:
- grad_image_head: float32 [1152, 1152], replicated
- grad_text_head: float32 [1152, 1152], replicated
Inputs may be any that keep to these rules, and one draw needn't show every extreme that they name: pair_ids never falls along the pairs; each id covers 1 to 8 consecutive pairs, and some id covers exactly 8.
All inputs are finite; a program needn't handle non-finite values.
Results may differ from a plain program's by a relative error of at most 0.0025.
Values may be sent and summed in bfloat16 or wider, within the bound.
No kernel may reach another device: no remote copies, remote signals or barrier semaphores. Data moves between devices by JAX's collectives and lax.ppermute only.
A program may use at most 128 MiB of HBM per device.

v0:
```python
import math

import jax
import jax.numpy as jnp
from jax import lax
from jax.sharding import PartitionSpec as P


def passed_along(value, axis, by):
    devices = lax.axis_size(axis)
    return lax.ppermute(value, axis, [(i, (i + by) % devices) for i in range(devices)])


def unit_rows(projected):
    length = jnp.sqrt(jnp.sum(projected * projected, axis=1, keepdims=True) + 1e-06)
    return (projected / length, length)


def unit_back(gradient, direction, length):
    radial = jnp.sum(gradient * direction, axis=1, keepdims=True)
    return ((gradient - radial * direction) / length).astype(jnp.bfloat16)


def local(image_embed, text_embed, image_head, text_head, pair_ids, logit_scale, logit_bias):
    tok_rows = image_embed.shape[0]
    dp_count = lax.axis_size("dp")
    inner_count = lax.axis_size("inner")
    loss_weight = 1.0 / math.sqrt(tok_rows * dp_count * inner_count)
    scale_value = logit_scale[0]
    bias_value = logit_bias[0]
    img_dir, img_length = unit_rows(
        jnp.dot(image_embed, image_head, preferred_element_type=jnp.float32)
    )
    txt_dir, txt_length = unit_rows(
        jnp.dot(text_embed, text_head, preferred_element_type=jnp.float32)
    )
    img_unit = img_dir.astype(jnp.bfloat16)
    txt_unit = txt_dir.astype(jnp.bfloat16)
    group_unit, group_ids = (
        lax.all_gather(img_unit, "inner", axis=0, tiled=True),
        lax.all_gather(pair_ids, "inner", axis=0, tiled=True),
    )

    def pair_tile(text_block, text_ids):
        logits = (
            scale_value
            * lax.dot_general(
                group_unit, text_block, (((1,), (1,)), ((), ())), preferred_element_type=jnp.float32
            )
            + bias_value
        )
        label_sign = jnp.where(group_ids[:, None] == text_ids[None, :], 1.0, -1.0).astype(
            jnp.float32
        )
        pair_coef = (
            -label_sign * jax.nn.sigmoid(-label_sign * logits) * scale_value * loss_weight
        ).astype(jnp.bfloat16)
        img_part = jnp.dot(pair_coef, text_block, preferred_element_type=jnp.float32)
        txt_part = lax.dot_general(
            pair_coef, group_unit, (((0,), (0,)), ((), ())), preferred_element_type=jnp.float32
        )
        return (img_part, txt_part)

    text_units = [txt_unit]
    text_ids = [pair_ids]
    carried_grads = [jnp.zeros(block.shape, jnp.float32) for block in text_units]
    owner_parts = None
    img_acc = jnp.zeros(group_unit.shape, jnp.float32)

    def visit_block(img_acc, text_units, text_ids, carried_grads, owner_parts):
        img_part, txt_part = pair_tile(text_units[0], text_ids[0])
        img_acc = img_acc + img_part
        new_grads = [carried_grads[0] + txt_part]
        return (img_acc, new_grads, owner_parts)

    def advance(turn_index, loop_state):
        img_acc, text_units, text_ids, carried_grads, owner_parts = loop_state
        img_acc, carried_grads, owner_parts = visit_block(
            img_acc, text_units, text_ids, carried_grads, owner_parts
        )
        ahead_pair = passed_along((text_units[0], text_ids[0]), "dp", 1)
        text_units = [ahead_pair[0]]
        text_ids = [ahead_pair[1]]
        carried_grads = [passed_along(carried_grads[0], "dp", 1)]
        return (img_acc, text_units, text_ids, carried_grads, owner_parts)

    loop_state = lax.fori_loop(
        0, dp_count - 1, advance, (img_acc, text_units, text_ids, carried_grads, owner_parts)
    )
    img_acc, text_units, text_ids, carried_grads, owner_parts = loop_state
    img_acc, carried_grads, owner_parts = visit_block(
        img_acc, text_units, text_ids, carried_grads, owner_parts
    )
    returned = passed_along(carried_grads[0], "dp", 1)
    img_grad = lax.psum_scatter(img_acc, "inner", scatter_dimension=0, tiled=True)
    img_back = unit_back(img_grad, img_dir, img_length)
    txt_back = unit_back(returned, txt_dir, txt_length)
    local_image = lax.dot_general(
        image_embed, img_back, (((0,), (0,)), ((), ())), preferred_element_type=jnp.float32
    )
    local_text = lax.dot_general(
        text_embed, txt_back, (((0,), (0,)), ((), ())), preferred_element_type=jnp.float32
    )
    grad_image_head, grad_text_head = lax.psum((local_image, local_text), ("dp", "inner"))
    return (grad_image_head, grad_text_head)


def solution(mesh):
    return jax.shard_map(
        local,
        mesh=mesh,
        in_specs=(
            P(("dp", "inner"), None),
            P(("dp", "inner"), None),
            P(),
            P(),
            P(("dp", "inner")),
            P(),
            P(),
        ),
        out_specs=(P(), P()),
        check_vma=False,
    )
```

profile of v0, /device:TPU:1, one launch (start us, length us, event | category | flops | bytes accessed | tf_op | source)
XLA Modules:
  0.0 686.4 jit_solution(11026157566144427650)
XLA Ops:
  13.6 21.1 %all-gather = s32[8,1,128]{2,1,0:T(1,128)S(1)} all-gather(s32[1,1,128]{2,1,0:T(1,128)S(1)} %bitcast.41), channel_id=1, replica_groups=mesh['dp'=16,'inner'=8] {'inner'}, dimensions={0}, use_global_device_ids=true | all-gather | bytes 4608 | tf_op jit(solution)/shard_map/all_gather | solution.py:41
  38.9 32.7 %all-gather.3.cloned.1.call-done = bf16[1024,1152]{1,0:T(8,128)(2,1)} async-done(((bf16[128,1152]{1,0:T(8,128)(2,1)}), bf16[1024,1152]{1,0:T(8,128)(2,1)}) %all-gather.3.cloned.1.call-update) | async-done | bytes 2359312 | tf_op jit(solution)/shard_map/all_gather | solution.py:40
  71.6 316.3 %while.17 = (s32[]{:T(128)}, f32[1024,1152]{1,0:T(8,128)}, bf16[128,1152]{1,0:T(8,128)(2,1)}, s32[128]{0:T(128)S(1)}, f32[128,1152]{1,0:T(8,128)S(1)}, /*index=5...) while((s32[]{:T(128)}, f32[1024,1152]{1,0:T(8,128)}, ...), condition=%wide.region_3.4_spmd.clone, body=%wide.region_2.3_spmd.clone.sunk | while | flops 910180352 | bytes 31334192 | solution.py:87
  201.7 5.4 convolution_add_fusion.6
  207.1 5.8 collective-permute-done.1
  223.5 5.4 convolution_add_fusion.6
  228.9 5.8 collective-permute-done.1
  245.4 5.4 convolution_add_fusion.6
  250.7 5.8 collective-permute-done.1
  267.2 5.4 convolution_add_fusion.6
  272.6 5.8 collective-permute-done.1
  289.0 5.4 convolution_add_fusion.6
  294.4 5.8 collective-permute-done.1
  310.9 5.4 convolution_add_fusion.6
  316.2 5.8 collective-permute-done.1
  332.7 5.4 convolution_add_fusion.6
  338.1 5.8 collective-permute-done.1
  359.9 5.8 collective-permute-done.1
  381.7 5.8 collective-permute-done.1
  397.8 14.3 %collective-permute-done.3 = f32[128,1152]{1,0:T(8,128)S(1)} collective-permute-done((f32[128,1152]{1,0:T(8,128)S(1)}, f32[128,1152]{1,0:T(8,128)S(1)}, u32[]{:S(2)}, u32[]{:S(2)}) %collective-permute-start.3) | collective-permute-done | bytes 589856 | tf_op jit(solution)/shard_map/ppermute | solution.py:11
  416.8 77.7 %reduce-scatter.2.cloned.1.call-done = f32[128,1152]{1,0:T(8,128)} async-done(((f32[1024,1152]{1,0:T(8,128)}), f32[128,1152]{1,0:T(8,128)}) %reduce-scatter.2.cloned.1.call-update) | async-done | bytes 589840 | tf_op jit(solution)/shard_map/reduce_scatter | solution.py:95
  500.3 165.9 %all-reduce.3.cloned.1.call-done = (f32[1152,1152]{0,1:T(8,128)}, f32[1152,1152]{0,1:T(8,128)}) async-done(((f32[1152,1152]{0,1:T(8,128)}, f32[1152,1152]{0,1:T(8,128)}), (f32[1152,1152]{0,1:T(8,128)}, f32[1152,1152]{0,1:T(8,128)})) %all-reduce.3.cloned.1.call-update) | async-done | bytes 10616848 | tf_op jit(solution)/shard_map/psum | solution.py:104
  666.2 6.9 copy.11
  673.0 6.9 copy.12
  (250 shorter events, 255.2 us)
Async XLA Ops:
  7.2 64.4 %all-gather.3.cloned.1.call-start = ((), (), s32[]{:S(2)}) async-start(), calls=%async_computation.1 | async-start | bytes 2654208 | tf_op jit(solution)/shard_map/all_gather | solution.py:40
  12.3 482.2 %reduce-scatter.2.cloned.1.call-start = ((), (), s32[]{:S(2)}) async-start(), calls=%async_computation.2 | async-start | bytes 5308416 | tf_op jit(solution)/shard_map/reduce_scatter | solution.py:95
  198.3 14.9 %collective-permute-start.2 = (f32[128,1152]{1,0:T(8,128)}, f32[128,1152]{1,0:T(8,128)S(1)}, u32[]{:S(2)}, u32[]{:S(2)}) collective-permute-start(f32[128,1152]{1,0:T(8,128)} %convolution_add_fusion.7), channel_id=1, source_target_pairs={{0,8},{8,16},{16,24},{24,32},{32,40},{40,48},{48,56},{56,64},{64,7... | collective-permute-start | bytes 1769480 | tf_op jit(solution)/shard_map/while/body/eval_jaxpr/ppermute | solution.py:11
  220.2 14.9 %collective-permute-start.2 = (f32[128,1152]{1,0:T(8,128)}, f32[128,1152]{1,0:T(8,128)S(1)}, u32[]{:S(2)}, u32[]{:S(2)}) collective-permute-start(f32[128,1152]{1,0:T(8,128)} %convolution_add_fusion.7), channel_id=1, source_target_pairs={{0,8},{8,16},{16,24},{24,32},{32,40},{40,48},{48,56},{56,64},{64,7... | collective-permute-start | bytes 1769480 | tf_op jit(solution)/shard_map/while/body/eval_jaxpr/ppermute | solution.py:11
  220.2 14.9 %collective-permute-start = (bf16[128,1152]{1,0:T(8,128)(2,1)S(1)}, bf16[128,1152]{1,0:T(8,128)(2,1)}, u32[]{:S(2)}, u32[]{:S(2)}) collective-permute-start(bf16[128,1152]{1,0:T(8,128)(2,1)S(1)} %copy.20), channel_id=1, source_target_pairs={{0,8},{8,16},{16,24},{24,32},{32,40},{40,48},{48,56},{56,64},{64,7... | collective-permute-start | bytes 884744 | tf_op jit(solution)/shard_map/while/body/eval_jaxpr/ppermute | solution.py:11
  242.0 14.9 %collective-permute-start.2 = (f32[128,1152]{1,0:T(8,128)}, f32[128,1152]{1,0:T(8,128)S(1)}, u32[]{:S(2)}, u32[]{:S(2)}) collective-permute-start(f32[128,1152]{1,0:T(8,128)} %convolution_add_fusion.7), channel_id=1, source_target_pairs={{0,8},{8,16},{16,24},{24,32},{32,40},{40,48},{48,56},{56,64},{64,7... | collective-permute-start | bytes 1769480 | tf_op jit(solution)/shard_map/while/body/eval_jaxpr/ppermute | solution.py:11
  242.0 14.6 %collective-permute-start.1 = (s32[128]{0:T(128)}, s32[128]{0:T(128)S(1)}, u32[]{:S(2)}, u32[]{:S(2)}) collective-permute-start(s32[128]{0:T(128)} %copy.21), channel_id=1, source_target_pairs={{0,8},{8,16},{16,24},{24,32},{32,40},{40,48},{48,56},{56,64},{64,7... | collective-permute-start | bytes 1544 | tf_op jit(solution)/shard_map/while/body/eval_jaxpr/ppermute | solution.py:11
  242.0 14.9 %collective-permute-start = (bf16[128,1152]{1,0:T(8,128)(2,1)S(1)}, bf16[128,1152]{1,0:T(8,128)(2,1)}, u32[]{:S(2)}, u32[]{:S(2)}) collective-permute-start(bf16[128,1152]{1,0:T(8,128)(2,1)S(1)} %copy.20), channel_id=1, source_target_pairs={{0,8},{8,16},{16,24},{24,32},{32,40},{40,48},{48,56},{56,64},{64,7... | collective-permute-start | bytes 884744 | tf_op jit(solution)/shard_map/while/body/eval_jaxpr/ppermute | solution.py:11
  263.8 14.9 %collective-permute-start.2 = (f32[128,1152]{1,0:T(8,128)}, f32[128,1152]{1,0:T(8,128)S(1)}, u32[]{:S(2)}, u32[]{:S(2)}) collective-permute-start(f32[128,1152]{1,0:T(8,128)} %convolution_add_fusion.7), channel_id=1, source_target_pairs={{0,8},{8,16},{16,24},{24,32},{32,40},{40,48},{48,56},{56,64},{64,7... | collective-permute-start | bytes 1769480 | tf_op jit(solution)/shard_map/while/body/eval_jaxpr/ppermute | solution.py:11
  263.8 14.9 %collective-permute-start = (bf16[128,1152]{1,0:T(8,128)(2,1)S(1)}, bf16[128,1152]{1,0:T(8,128)(2,1)}, u32[]{:S(2)}, u32[]{:S(2)}) collective-permute-start(bf16[128,1152]{1,0:T(8,128)(2,1)S(1)} %copy.20), channel_id=1, source_target_pairs={{0,8},{8,16},{16,24},{24,32},{32,40},{40,48},{48,56},{56,64},{64,7... | collective-permute-start | bytes 884744 | tf_op jit(solution)/shard_map/while/body/eval_jaxpr/ppermute | solution.py:11
  285.7 14.9 %collective-permute-start.2 = (f32[128,1152]{1,0:T(8,128)}, f32[128,1152]{1,0:T(8,128)S(1)}, u32[]{:S(2)}, u32[]{:S(2)}) collective-permute-start(f32[128,1152]{1,0:T(8,128)} %convolution_add_fusion.7), channel_id=1, source_target_pairs={{0,8},{8,16},{16,24},{24,32},{32,40},{40,48},{48,56},{56,64},{64,7... | collective-permute-start | bytes 1769480 | tf_op jit(solution)/shard_map/while/body/eval_jaxpr/ppermute | solution.py:11
  285.7 14.6 %collective-permute-start.1 = (s32[128]{0:T(128)}, s32[128]{0:T(128)S(1)}, u32[]{:S(2)}, u32[]{:S(2)}) collective-permute-start(s32[128]{0:T(128)} %copy.21), channel_id=1, source_target_pairs={{0,8},{8,16},{16,24},{24,32},{32,40},{40,48},{48,56},{56,64},{64,7... | collective-permute-start | bytes 1544 | tf_op jit(solution)/shard_map/while/body/eval_jaxpr/ppermute | solution.py:11
  285.7 14.9 %collective-permute-start = (bf16[128,1152]{1,0:T(8,128)(2,1)S(1)}, bf16[128,1152]{1,0:T(8,128)(2,1)}, u32[]{:S(2)}, u32[]{:S(2)}) collective-permute-start(bf16[128,1152]{1,0:T(8,128)(2,1)S(1)} %copy.20), channel_id=1, source_target_pairs={{0,8},{8,16},{16,24},{24,32},{32,40},{40,48},{48,56},{56,64},{64,7... | collective-permute-start | bytes 884744 | tf_op jit(solution)/shard_map/while/body/eval_jaxpr/ppermute | solution.py:11
  307.5 14.9 %collective-permute-start.2 = (f32[128,1152]{1,0:T(8,128)}, f32[128,1152]{1,0:T(8,128)S(1)}, u32[]{:S(2)}, u32[]{:S(2)}) collective-permute-start(f32[128,1152]{1,0:T(8,128)} %convolution_add_fusion.7), channel_id=1, source_target_pairs={{0,8},{8,16},{16,24},{24,32},{32,40},{40,48},{48,56},{56,64},{64,7... | collective-permute-start | bytes 1769480 | tf_op jit(solution)/shard_map/while/body/eval_jaxpr/ppermute | solution.py:11
  307.5 14.9 %collective-permute-start = (bf16[128,1152]{1,0:T(8,128)(2,1)S(1)}, bf16[128,1152]{1,0:T(8,128)(2,1)}, u32[]{:S(2)}, u32[]{:S(2)}) collective-permute-start(bf16[128,1152]{1,0:T(8,128)(2,1)S(1)} %copy.20), channel_id=1, source_target_pairs={{0,8},{8,16},{16,24},{24,32},{32,40},{40,48},{48,56},{56,64},{64,7... | collective-permute-start | bytes 884744 | tf_op jit(solution)/shard_map/while/body/eval_jaxpr/ppermute | solution.py:11
  329.3 14.9 %collective-permute-start.2 = (f32[128,1152]{1,0:T(8,128)}, f32[128,1152]{1,0:T(8,128)S(1)}, u32[]{:S(2)}, u32[]{:S(2)}) collective-permute-start(f32[128,1152]{1,0:T(8,128)} %convolution_add_fusion.7), channel_id=1, source_target_pairs={{0,8},{8,16},{16,24},{24,32},{32,40},{40,48},{48,56},{56,64},{64,7... | collective-permute-start | bytes 1769480 | tf_op jit(solution)/shard_map/while/body/eval_jaxpr/ppermute | solution.py:11
  329.3 14.6 %collective-permute-start.1 = (s32[128]{0:T(128)}, s32[128]{0:T(128)S(1)}, u32[]{:S(2)}, u32[]{:S(2)}) collective-permute-start(s32[128]{0:T(128)} %copy.21), channel_id=1, source_target_pairs={{0,8},{8,16},{16,24},{24,32},{32,40},{40,48},{48,56},{56,64},{64,7... | collective-permute-start | bytes 1544 | tf_op jit(solution)/shard_map/while/body/eval_jaxpr/ppermute | solution.py:11
  329.3 14.9 %collective-permute-start = (bf16[128,1152]{1,0:T(8,128)(2,1)S(1)}, bf16[128,1152]{1,0:T(8,128)(2,1)}, u32[]{:S(2)}, u32[]{:S(2)}) collective-permute-start(bf16[128,1152]{1,0:T(8,128)(2,1)S(1)} %copy.20), channel_id=1, source_target_pairs={{0,8},{8,16},{16,24},{24,32},{32,40},{40,48},{48,56},{56,64},{64,7... | collective-permute-start | bytes 884744 | tf_op jit(solution)/shard_map/while/body/eval_jaxpr/ppermute | solution.py:11
  351.2 14.9 %collective-permute-start.2 = (f32[128,1152]{1,0:T(8,128)}, f32[128,1152]{1,0:T(8,128)S(1)}, u32[]{:S(2)}, u32[]{:S(2)}) collective-permute-start(f32[128,1152]{1,0:T(8,128)} %convolution_add_fusion.7), channel_id=1, source_target_pairs={{0,8},{8,16},{16,24},{24,32},{32,40},{40,48},{48,56},{56,64},{64,7... | collective-permute-start | bytes 1769480 | tf_op jit(solution)/shard_map/while/body/eval_jaxpr/ppermute | solution.py:11
  351.2 14.9 %collective-permute-start = (bf16[128,1152]{1,0:T(8,128)(2,1)S(1)}, bf16[128,1152]{1,0:T(8,128)(2,1)}, u32[]{:S(2)}, u32[]{:S(2)}) collective-permute-start(bf16[128,1152]{1,0:T(8,128)(2,1)S(1)} %copy.20), channel_id=1, source_target_pairs={{0,8},{8,16},{16,24},{24,32},{32,40},{40,48},{48,56},{56,64},{64,7... | collective-permute-start | bytes 884744 | tf_op jit(solution)/shard_map/while/body/eval_jaxpr/ppermute | solution.py:11
  373.0 14.9 %collective-permute-start.2 = (f32[128,1152]{1,0:T(8,128)}, f32[128,1152]{1,0:T(8,128)S(1)}, u32[]{:S(2)}, u32[]{:S(2)}) collective-permute-start(f32[128,1152]{1,0:T(8,128)} %convolution_add_fusion.7), channel_id=1, source_target_pairs={{0,8},{8,16},{16,24},{24,32},{32,40},{40,48},{48,56},{56,64},{64,7... | collective-permute-start | bytes 1769480 | tf_op jit(solution)/shard_map/while/body/eval_jaxpr/ppermute | solution.py:11
  373.0 14.6 %collective-permute-start.1 = (s32[128]{0:T(128)}, s32[128]{0:T(128)S(1)}, u32[]{:S(2)}, u32[]{:S(2)}) collective-permute-start(s32[128]{0:T(128)} %copy.21), channel_id=1, source_target_pairs={{0,8},{8,16},{16,24},{24,32},{32,40},{40,48},{48,56},{56,64},{64,7... | collective-permute-start | bytes 1544 | tf_op jit(solution)/shard_map/while/body/eval_jaxpr/ppermute | solution.py:11
  373.0 14.9 %collective-permute-start = (bf16[128,1152]{1,0:T(8,128)(2,1)S(1)}, bf16[128,1152]{1,0:T(8,128)(2,1)}, u32[]{:S(2)}, u32[]{:S(2)}) collective-permute-start(bf16[128,1152]{1,0:T(8,128)(2,1)S(1)} %copy.20), channel_id=1, source_target_pairs={{0,8},{8,16},{16,24},{24,32},{32,40},{40,48},{48,56},{56,64},{64,7... | collective-permute-start | bytes 884744 | tf_op jit(solution)/shard_map/while/body/eval_jaxpr/ppermute | solution.py:11
  395.3 270.9 %all-reduce.3.cloned.1.call-start = ((), (), s32[]{:S(2)}) async-start(), calls=%async_computation.3 | async-start | bytes 21233664 | tf_op jit(solution)/shard_map/psum | solution.py:104
  (64 other events, 578.2 us)
Sparse Core Ops, SparseCore 0:
  12.4 59.1 all-gather.2
  395.4 99.0 reduce-scatter.1
  501.1 165.0 all-reduce.2
where the time goes:
time: 688 us; the launch traced here: 686 us
  waiting for transfers between devices  368 us (53%)
  matrix products  178 us (26%)
  starting transfers between devices  55.6 us (8%)
  local copies, waits for them, and re-layouts  43 us (6%)
  blocking collectives  21.1 us (3%)
  between operations  15.2 us (2%)
    psum x1, waiting for transfers between devices, local(): lax.psum((local_image, local_text), ('dp', 'inner'))  166 us
    ppermute x46, waiting for transfers between devices, passed_along(): lax.ppermute(value, axis, [(i, (i + by) % devices) for i in range(devices)])  92 us
    dot_general x16, matrix products, pair_tile(): jnp.dot(pair_coef, text_block, preferred_element_type=jnp.float32)  83.1 us
    reduce_scatter x1, waiting for transfers between devices, local(): lax.psum_scatter(img_acc, 'inner', scatter_dimension=0, tiled=True)  77.7 us
    dot_general x16, matrix products, pair_tile(): lax.dot_general(group_unit, text_block, (((1,), (1,)), ((), ())), preferr...  60.8 us
    ppermute x46, starting transfers between devices, passed_along(): lax.ppermute(value, axis, [(i, (i + by) % devices) for i in range(devices)])  55.5 us
    all_gather x1, waiting for transfers between devices, local(): lax.all_gather(img_unit, 'inner', axis=0, tiled=True)  32.7 us
    while x90, local copies, waits for them, and re-layouts  25.2 us
  transfers between devices with their start and end apart: 49, of which 34 were waited for; matrix products, arithmetic and copies ran while one was open for 13% of the time, Pallas kernels for 0%

commit v1 on v0

v1 whole, which is shorter than its diff:
```python
import math

import jax
import jax.numpy as jnp
from jax import lax
from jax.sharding import Mesh, PartitionSpec as P

AXES = ("zl", "y", "c", "x", "zh")
SIZES = (2, 4, 2, 4, 2)
BF16 = jnp.bfloat16
F32 = jnp.float32


def routes(move):
    pairs = []
    index = 0
    for zl in range(2):
        for y in range(4):
            for c in range(2):
                for x in range(4):
                    for zh in range(2):
                        tzl, ty, tc, tx, tzh = move(zl, y, c, x, zh)
                        pairs.append((index, (((tzl * 4 + ty) * 2 + tc) * 4 + tx) * 2 + tzh))
                        index += 1
    return pairs


def send(value, move):
    return lax.ppermute(value, AXES, routes(move))


def other_core(zl, y, c, x, zh):
    return (zl, y, 1 - c, x, zh)


def z_pair(swap):
    def move(zl, y, c, x, zh):
        return (1 - zl, y, c, x, zh if (c ^ swap) == 0 else 1 - zh)

    return move


def ring(by, swap):
    def move(zl, y, c, x, zh):
        if (c ^ swap) == 0:
            return (zl, y, c, (x + by) % 4, zh)
        return (zl, (y + by) % 4, c, x, zh)

    return move


def z_ring(by):
    def move(zl, y, c, x, zh):
        z = (zh * 2 + zl + by) % 4
        return (z % 2, y, c, x, z // 2)

    return move


def with_partner(value, swap):
    got = send(value, z_pair(swap))
    return jnp.concatenate([value[:128], got[:128], value[128:129], got[128:129], value[130:144]], axis=0)


def unit_rows(projected):
    length = jnp.sqrt(jnp.sum(projected * projected, axis=1, keepdims=True) + 1e-06)
    return (projected / length, length)


def block_ids(blocks):
    rows = jnp.concatenate([block[256:258, :256].astype(F32) for block in blocks], axis=0)
    return (rows[:, :128] * 64.0 + rows[:, 128:]).reshape(-1)


def scattered(value, by_route, mine, kind):
    rows = value.shape[0] // 4
    total = lax.dynamic_slice_in_dim(value, mine * rows, rows, 0)
    parts = []
    for by in (1, 3, 2):
        part = lax.dynamic_slice_in_dim(value, lax.rem(mine + by, 4) * rows, rows, 0).astype(kind)
        parts.append(send(part, by_route(by)))
    for part in parts:
        total = total + part.astype(F32)
    return total


def gathered(value, by_route, mine):
    rows = value.shape[0]
    out = jnp.zeros((4 * rows,) + value.shape[1:], value.dtype)
    parts = [(0, value)] + [(by, send(value, by_route(by))) for by in (1, 3, 2)]
    for by, part in parts:
        out = lax.dynamic_update_slice_in_dim(out, part, lax.rem(mine + 4 - by, 4) * rows, 0)
    return out


def local(image_embed, text_embed, image_head, text_head, pair_ids, logit_scale, logit_bias):
    core = lax.axis_index("c")
    first = core == 0
    scale = logit_scale[0]
    bias = logit_bias[0]
    weight = 1.0 / math.sqrt(16384)

    ids_row = jnp.concatenate(
        [(pair_ids // 64).astype(BF16), (pair_ids % 64).astype(BF16), jnp.zeros((896,), BF16)]
    )[None]
    ids_rows = jnp.concatenate([ids_row, jnp.zeros((15, 1152), BF16)], axis=0)
    mine = jnp.concatenate([jnp.where(first, image_embed, text_embed), ids_rows], axis=0)
    theirs = jnp.concatenate([jnp.where(first, text_embed, image_embed), ids_rows], axis=0)
    head_mine = jnp.where(first, image_head, text_head)
    head_theirs = jnp.where(first, text_head, image_head)

    mine = with_partner(mine, 0)
    theirs = with_partner(theirs, 1)
    mine_blocks = [mine]
    theirs_blocks = [theirs]
    for by in (1, 3, 2):
        mine_blocks.append(send(mine, ring(by, 0)))
        theirs_blocks.append(send(theirs, ring(by, 1)))
    mine_over = [send(block, other_core) for block in theirs_blocks]
    theirs_over = [send(block, other_core) for block in mine_blocks]
    mine_blocks = mine_blocks + mine_over
    theirs_blocks = theirs_blocks + theirs_over

    rows_mine = jnp.concatenate([block[:256] for block in mine_blocks], axis=0)
    rows_theirs = jnp.concatenate([block[:256] for block in theirs_blocks], axis=0)
    ids_mine = block_ids(mine_blocks)
    ids_theirs = block_ids(theirs_blocks)

    dir_mine, length_mine = unit_rows(jnp.dot(rows_mine, head_mine, preferred_element_type=F32))
    dir_theirs, _ = unit_rows(jnp.dot(rows_theirs, head_theirs, preferred_element_type=F32))
    unit_mine = dir_mine.astype(BF16)
    unit_theirs = dir_theirs.astype(BF16)
    logits = (
        scale
        * lax.dot_general(
            unit_mine, unit_theirs, (((1,), (1,)), ((), ())), preferred_element_type=F32
        )
        + bias
    )
    sign = jnp.where(ids_mine[:, None] == ids_theirs[None, :], 1.0, -1.0)
    coef = (-sign * jax.nn.sigmoid(-sign * logits) * scale * weight).astype(BF16)
    grad = jnp.dot(coef, unit_theirs, preferred_element_type=F32)
    radial = jnp.sum(grad * dir_mine, axis=1, keepdims=True)
    back = ((grad - radial * dir_mine) / length_mine).astype(BF16)
    part = lax.dot_general(rows_mine, back, (((0,), (0,)), ((), ())), preferred_element_type=F32)

    at_x = lax.axis_index("x")
    at_y = lax.axis_index("y")
    at_first = jnp.where(first, at_x, at_y)
    at_second = jnp.where(first, at_y, at_x)
    part = scattered(part, lambda by: ring(by, 0), at_first, BF16)
    part = scattered(part, lambda by: ring(by, 1), at_second, F32)
    moved = [send(part, z_ring(by)) for by in (1, 3, 2)]
    at_z = lax.axis_index("zh") * 2 + lax.axis_index("zl")
    stack = jnp.zeros((4,) + part.shape, F32)
    for by, piece in zip((0, 1, 3, 2), [part] + moved):
        stack = lax.dynamic_update_slice_in_dim(stack, piece[None], lax.rem(at_z + 4 - by, 4), 0)
    part = (stack[0] + stack[1]) + (stack[2] + stack[3])
    part = gathered(part, lambda by: ring(by, 1), at_second)
    whole = gathered(part, lambda by: ring(by, 0), at_first)
    other = send(whole, other_core)
    return (jnp.where(first, whole, other), jnp.where(first, other, whole))


def solution(mesh):
    split = Mesh(mesh.devices.reshape(SIZES), AXES)
    every = P(AXES)
    return jax.shard_map(
        local,
        mesh=split,
        in_specs=(every, every, P(), P(), every, P(), P()),
        out_specs=(P(), P()),
        check_vma=False,
    )
```

time: 688 us -> 258 us (0.38)
  waiting for transfers between devices: 368 us -> 80.7 us
  matrix products: 178 us -> 69.7 us
  blocking collectives: 21.1 us -> 0 us
  local copies, waits for them, and re-layouts: 43 us -> 28.6 us
  between operations: 15.2 us -> 2.38 us
  starting transfers between devices: 55.6 us -> 65.1 us
    psum x1 -> x0, waiting for transfers between devices: 166 us -> none  [local(): lax.psum((local_image, local_text), ('dp', 'inner'))]
    dot_general x52 -> x4, matrix products: 178 us -> 69.7 us  [the longest x1 37.1 us: local(): grad = jnp.dot(coef, unit_theirs, preferred_element_type=F32)]
    reduce_scatter x1 -> x0, waiting for transfers between devices: 77.7 us -> none  [local(): lax.psum_scatter(img_acc, 'inner', scatter_dimension=0, tiled=True)]
    all_gather x1 -> x0, waiting for transfers between devices: 32.7 us -> none  [local(): lax.all_gather(img_unit, 'inner', axis=0, tiled=True)]
    while x90 -> x0, local copies, waits for them, and re-layouts: 25.2 us -> none
    all_gather x1 -> x0, blocking collectives: 21.1 us -> none  [local(): lax.all_gather(pair_ids, 'inner', axis=0, tiled=True)]
    ppermute x46 -> x32, waiting for transfers between devices: 92 us -> 80.7 us  [send(): return lax.ppermute(value, AXES, routes(move))]
    ppermute x46 -> x32, starting transfers between devices: 55.5 us -> 65.1 us  [send(): return lax.ppermute(value, AXES, routes(move))]
  transfers between devices with their start and end apart: 49 -> 32, of which waited for: 34 -> 16; matrix products, arithmetic and copies ran while one was open for 13% -> 8% of each run, Pallas kernels for 0% -> 0%
where the time goes in v1:
time: 258 us; the launch traced here: 257 us
  waiting for transfers between devices  80.7 us (31%)
  matrix products  69.7 us (27%)
  starting transfers between devices  65.1 us (25%)
  local copies, waits for them, and re-layouts  28.6 us (11%)
  other arithmetic  10.7 us (4%)
    ppermute x32, waiting for transfers between devices, send(): return lax.ppermute(value, AXES, routes(move))  80.7 us
    ppermute x32, starting transfers between devices, send(): return lax.ppermute(value, AXES, routes(move))  65.1 us
    dot_general x1, matrix products, local(): grad = jnp.dot(coef, unit_theirs, preferred_element_type=F32)  37.1 us
    unnamed x37, local copies, waits for them, and re-layouts  16.1 us
    dot_general x1, matrix products, local(): lax.dot_general(rows_mine, back, (((0,), (0,)), ((), ())), preferred_elem...  12.4 us
    dot_general x1, matrix products, local(): jnp.dot(rows_theirs, head_theirs, preferred_element_type=F32)  11.3 us
    dot_general x1, matrix products, local(): jnp.dot(rows_mine, head_mine, preferred_element_type=F32)  8.9 us
  transfers between devices with their start and end apart: 32, of which 16 were waited for; matrix products, arithmetic and copies ran while one was open for 8% of the time, Pallas kernels for 0%

profile of v1, /device:TPU:1, one launch (start us, length us, event | category | flops | bytes accessed | tf_op | source)
XLA Modules:
  0.0 257.3 jit_solution(13040496993590445071)
XLA Ops:
  3.6 2.5 collective-permute-start.4
  6.1 2.2 collective-permute-start
  22.7 2.9 %collective-permute-start.3 = (bf16[272,1152]{1,0:T(8,128)(2,1)S(1)}, bf16[272,1152]{1,0:T(8,128)(2,1)}, u32[]{:S(2)}, u32[]{:S(2)}) collective-permute-start(bf16[272,1152]{1,0:T(8,128)(2,1)S(1)} %concatenate.48), channel_id=1, source_target_pairs={{0,4},{1,5},{2,6},{3,7},{4,0},{5,1},{6,2},{7,3},{8,40},{9,41},{10,... | collective-permute-start | bytes 1880072 | tf_op jit(solution)/shard_map/ppermute | solution.py:29
  27.6 14.1 %collective-permute-start.5 = (bf16[272,1152]{1,0:T(8,128)(2,1)S(1)}, bf16[272,1152]{1,0:T(8,128)(2,1)S(1)}, u32[]{:S(2)}, u32[]{:S(2)}) collective-permute-start(bf16[272,1152]{1,0:T(8,128)(2,1)S(1)} %concatenate.50), channel_id=1, source_target_pairs={{0,8},{1,9},{2,10},{3,11},{4,12},{5,13},{6,14},{7,15},{8,0},{9,1},... | collective-permute-start | bytes 1880072 | tf_op jit(solution)/shard_map/ppermute | solution.py:29
  42.5 8.8 %collective-permute-start.12 = (bf16[272,1152]{1,0:T(8,128)(2,1)S(1)}, bf16[272,1152]{1,0:T(8,128)(2,1)S(1)}, u32[]{:S(2)}, u32[]{:S(2)}) collective-permute-start(bf16[272,1152]{1,0:T(8,128)(2,1)S(1)} %concatenate.48), channel_id=1, source_target_pairs={{0,8},{1,9},{2,10},{3,11},{4,12},{5,13},{6,14},{7,15},{8,0},{9,1},... | collective-permute-start | bytes 1880072 | tf_op jit(solution)/shard_map/ppermute | solution.py:29
  68.0 11.3 %multiply_reduce_fusion.1 = (f32[2048]{0:T(1024)S(1)}, f32[2048,1152]{0,1:T(8,128)}) fusion(bf16[2048,1152]{1,0:T(8,128)(2,1)} %slice_dynamic-update-slice_fusion, bf16[1152,1152]{1,0:T(8,128)(2,1)} %param.10, bf16[1152,1152]{1,0:T(8,128)(2,1)} %param.9, pred[]{:T(512)S(6)} %eq.22), kind=kOutput, calls=%fused_computation.4 | convolution fusion | flops 5441861632 | bytes 19472384 | tf_op jit(solution)/shard_map/dot_general | solution.py:130
  79.6 8.9 %multiply_reduce_fusion.2 = (f32[2048]{0:T(1024)S(1)}, f32[2048,1152]{0,1:T(8,128)}) fusion(bf16[2048,1152]{1,0:T(8,128)(2,1)S(1)} %slice_dynamic-update-slice_fusion.7, bf16[1152,1152]{1,0:T(8,128)(2,1)S(1)} %copy-done.8, bf16[1152,1152]{1,0:T(8,128)(2,1)S(1)} %copy-done.9, pred[]{:T(512)S(6)} %eq.22), kind=kOutput, calls=%fused_computation.5 | convolution fusion | flops 5441861632 | bytes 19472384 | tf_op jit(solution)/shard_map/dot_general | solution.py:129
  88.6 37.1 %multiply_reduce_fusion = (f32[2048]{0:T(1024)S(1)}, f32[2048,1152]{0,1:T(8,128)}) fusion(f32[2048,1152]{0,1:T(8,128)} %get-tuple-element.33, f32[2048]{0:T(1024)S(1)} %get-tuple-element.39, f32[2048,1152]{0,1:T(8,128)} %get-tuple-element.31, f32[2048]{0:T(1024)S(1)} %get-tuple-element.38, f32[]{:T(128)} %bitcast.21, f32[]{:T(128)} %bitcast.20, ...), kind=kOutput, calls=%fused_computation.2 | convolution fusion | flops 19403110400 | bytes 28352520 | tf_op jit(solution)/shard_map/dot_general | solution.py:142
  125.7 12.4 %fusion.12 = f32[1152,1152]{1,0:T(8,128)S(1)} fusion(bf16[2048,1152]{1,0:T(8,128)(2,1)} %copy-done.7, f32[2048,1152]{0,1:T(8,128)} %get-tuple-element.35, f32[2048]{0:T(1024)S(1)} %get-tuple-element.34, f32[2048]{0:T(1024)S(1)} %get-tuple-element.39, f32[2048,1152]{0,1:T(8,128)} %get-tuple-element.33), kind=kOutput, calls=%fused_computation.17 | convolution fusion | flops 5447614464 | bytes 28917760 | tf_op jit(solution)/shard_map/dot_general | solution.py:145
  138.1 2.4 copy-done
  144.0 7.8 %collective-permute-done.16 = bf16[288,1152]{1,0:T(8,128)(2,1)S(1)} collective-permute-done((bf16[288,1152]{1,0:T(8,128)(2,1)S(1)}, bf16[288,1152]{1,0:T(8,128)(2,1)S(1)}, u32[]{:S(2)}, u32[]{:S(2)}) %collective-permute-start.16) | collective-permute-done | bytes 663584 | tf_op jit(solution)/shard_map/ppermute | solution.py:29
  151.9 7.4 %collective-permute-done.18 = bf16[288,1152]{1,0:T(8,128)(2,1)} collective-permute-done((bf16[288,1152]{1,0:T(8,128)(2,1)S(1)}, bf16[288,1152]{1,0:T(8,128)(2,1)}, u32[]{:S(2)}, u32[]{:S(2)}) %collective-permute-start.18) | collective-permute-done | bytes 663584 | tf_op jit(solution)/shard_map/ppermute | solution.py:29
  165.2 3.6 %collective-permute-done.19 = f32[72,1152]{1,0:T(8,128)S(1)} collective-permute-done((f32[72,1152]{1,0:T(8,128)S(1)}, f32[72,1152]{1,0:T(8,128)S(1)}, u32[]{:S(2)}, u32[]{:S(2)}) %collective-permute-start.19) | collective-permute-done | bytes 331808 | tf_op jit(solution)/shard_map/ppermute | solution.py:29
  168.8 2.8 %collective-permute-done.20 = f32[72,1152]{1,0:T(8,128)} collective-permute-done((f32[72,1152]{1,0:T(8,128)S(1)}, f32[72,1152]{1,0:T(8,128)}, u32[]{:S(2)}, u32[]{:S(2)}) %collective-permute-start.20) | collective-permute-done | bytes 331808 | tf_op jit(solution)/shard_map/ppermute | solution.py:29
  175.1 2.6 %collective-permute-start.23 = (f32[72,1152]{1,0:T(8,128)S(1)}, f32[72,1152]{1,0:T(8,128)S(1)}, u32[]{:S(2)}, u32[]{:S(2)}) collective-permute-start(f32[72,1152]{1,0:T(8,128)S(1)} %get-tuple-element.5), channel_id=1, source_target_pairs={{0,65},{1,64},{2,67},{3,66},{4,69},{5,68},{6,71},{7,70},{8,73},{9,... | collective-permute-start | bytes 995336 | tf_op jit(solution)/shard_map/ppermute | solution.py:29
  177.7 7.3 %collective-permute-done.22 = f32[72,1152]{1,0:T(8,128)S(1)} collective-permute-done((f32[72,1152]{1,0:T(8,128)S(1)}, f32[72,1152]{1,0:T(8,128)S(1)}, u32[]{:S(2)}, u32[]{:S(2)}) %collective-permute-start.22) | collective-permute-done | bytes 331808 | tf_op jit(solution)/shard_map/ppermute | solution.py:29
  185.0 4.2 %collective-permute-done.24 = f32[72,1152]{1,0:T(8,128)S(1)} collective-permute-done((f32[72,1152]{1,0:T(8,128)S(1)}, f32[72,1152]{1,0:T(8,128)S(1)}, u32[]{:S(2)}, u32[]{:S(2)}) %collective-permute-start.24) | collective-permute-done | bytes 331808 | tf_op jit(solution)/shard_map/ppermute | solution.py:29
  192.4 4.3 %collective-permute-done.25 = f32[72,1152]{1,0:T(8,128)S(1)} collective-permute-done((f32[72,1152]{1,0:T(8,128)S(1)}, f32[72,1152]{1,0:T(8,128)S(1)}, u32[]{:S(2)}, u32[]{:S(2)}) %collective-permute-start.25) | collective-permute-done | bytes 331808 | tf_op jit(solution)/shard_map/ppermute | solution.py:29
  196.8 3.1 %collective-permute-done.26 = f32[72,1152]{1,0:T(8,128)S(1)} collective-permute-done((f32[72,1152]{1,0:T(8,128)S(1)}, f32[72,1152]{1,0:T(8,128)S(1)}, u32[]{:S(2)}, u32[]{:S(2)}) %collective-permute-start.26) | collective-permute-done | bytes 331808 | tf_op jit(solution)/shard_map/ppermute | solution.py:29
  204.4 16.2 %collective-permute-done.28 = f32[288,1152]{1,0:T(8,128)} collective-permute-done((f32[288,1152]{1,0:T(8,128)S(1)}, f32[288,1152]{1,0:T(8,128)}, u32[]{:S(2)}, u32[]{:S(2)}) %collective-permute-start.28) | collective-permute-done | bytes 1327136 | tf_op jit(solution)/shard_map/ppermute | solution.py:29
  222.0 11.4 %collective-permute-done.29 = f32[288,1152]{1,0:T(8,128)} collective-permute-done((f32[288,1152]{1,0:T(8,128)S(1)}, f32[288,1152]{1,0:T(8,128)}, u32[]{:S(2)}, u32[]{:S(2)}) %collective-permute-start.29) | collective-permute-done | bytes 1327136 | tf_op jit(solution)/shard_map/ppermute | solution.py:29
  234.9 9.2 %collective-permute-start.31 = (f32[1152,1152]{1,0:T(8,128)S(1)}, f32[1152,1152]{1,0:T(8,128)S(1)}, u32[]{:S(2)}, u32[]{:S(2)}) collective-permute-start(f32[1152,1152]{1,0:T(8,128)S(1)} %constant_dynamic-update-slice_fusion.4), channel_id=1, source_target_pairs={{0,8},{1,9},{2,10},{3,11},{4,12},{5,13},{6,14},{7,15},{8,0},{9,1},... | collective-permute-start | bytes 15925256 | tf_op jit(solution)/shard_map/ppermute | solution.py:29
  244.1 8.4 %collective-permute-done.31 = f32[1152,1152]{1,0:T(8,128)S(1)} collective-permute-done((f32[1152,1152]{1,0:T(8,128)S(1)}, f32[1152,1152]{1,0:T(8,128)S(1)}, u32[]{:S(2)}, u32[]{:S(2)}) %collective-permute-start.31) | collective-permute-done | bytes 5308448 | tf_op jit(solution)/shard_map/ppermute | solution.py:29
  252.5 4.8 %broadcast_select_fusion = (f32[1152,1152]{1,0:T(8,128)}, f32[1152,1152]{1,0:T(8,128)}) fusion(f32[1152,1152]{1,0:T(8,128)S(1)} %collective-permute-done.31, f32[1152,1152]{1,0:T(8,128)S(1)} %constant_dynamic-update-slice_fusion.4, pred[]{:T(512)S(6)} %eq.22), kind=kLoop, calls=%fused_computation.22 | loop fusion | flops 2654208 | bytes 21233664 | tf_op jit(solution)/shard_map/jit(_where)/select_n | solution.py:162
  (139 shorter events, 59.1 us)
Async XLA Ops:
  6.1 10.7 %collective-permute-start = (bf16[144,1152]{1,0:T(8,128)(2,1)S(1)}, bf16[144,1152]{1,0:T(8,128)(2,1)}, u32[]{:S(2)}, u32[]{:S(2)}) collective-permute-start(bf16[144,1152]{1,0:T(8,128)(2,1)S(1)} %get-tuple-element.27), channel_id=1, source_target_pairs={{0,64},{1,65},{2,66},{3,67},{4,68},{5,69},{6,70},{7,71},{8,73},{9,... | collective-permute-start | bytes 995336 | tf_op jit(solution)/shard_map/ppermute | solution.py:29
  12.2 10.5 %collective-permute-start.6 = (bf16[272,1152]{1,0:T(8,128)(2,1)S(1)}, bf16[272,1152]{1,0:T(8,128)(2,1)}, u32[]{:S(2)}, u32[]{:S(2)}) collective-permute-start(bf16[272,1152]{1,0:T(8,128)(2,1)S(1)} %concatenate.50), channel_id=1, source_target_pairs={{0,16},{1,17},{2,18},{3,19},{4,20},{5,21},{6,22},{7,23},{8,10},{9,... | collective-permute-start | bytes 1880072 | tf_op jit(solution)/shard_map/ppermute | solution.py:29
  13.5 14.1 %collective-permute-start.8 = (bf16[272,1152]{1,0:T(8,128)(2,1)S(1)}, bf16[272,1152]{1,0:T(8,128)(2,1)S(1)}, u32[]{:S(2)}, u32[]{:S(2)}) collective-permute-start(bf16[272,1152]{1,0:T(8,128)(2,1)S(1)} %concatenate.50), channel_id=1, source_target_pairs={{0,48},{1,49},{2,50},{3,51},{4,52},{5,53},{6,54},{7,55},{8,14},{9,... | collective-permute-start | bytes 1880072 | tf_op jit(solution)/shard_map/ppermute | solution.py:29
  15.0 27.5 %collective-permute-start.10 = (bf16[272,1152]{1,0:T(8,128)(2,1)S(1)}, bf16[272,1152]{1,0:T(8,128)(2,1)S(1)}, u32[]{:S(2)}, u32[]{:S(2)}) collective-permute-start(bf16[272,1152]{1,0:T(8,128)(2,1)S(1)} %concatenate.50), channel_id=1, source_target_pairs={{0,32},{1,33},{2,34},{3,35},{4,36},{5,37},{6,38},{7,39},{8,12},{9,... | collective-permute-start | bytes 1880072 | tf_op jit(solution)/shard_map/ppermute | solution.py:29
  19.8 32.4 %collective-permute-start.1 = (bf16[272,1152]{1,0:T(8,128)(2,1)S(1)}, bf16[272,1152]{1,0:T(8,128)(2,1)}, u32[]{:S(2)}, u32[]{:S(2)}) collective-permute-start(bf16[272,1152]{1,0:T(8,128)(2,1)S(1)} %concatenate.48), channel_id=1, source_target_pairs={{0,2},{1,3},{2,4},{3,5},{4,6},{5,7},{6,0},{7,1},{8,24},{9,25},{10,... | collective-permute-start | bytes 1880072 | tf_op jit(solution)/shard_map/ppermute | solution.py:29
  21.2 33.0 %collective-permute-start.2 = (bf16[272,1152]{1,0:T(8,128)(2,1)S(1)}, bf16[272,1152]{1,0:T(8,128)(2,1)S(1)}, u32[]{:S(2)}, u32[]{:S(2)}) collective-permute-start(bf16[272,1152]{1,0:T(8,128)(2,1)S(1)} %concatenate.48), channel_id=1, source_target_pairs={{0,6},{1,7},{2,0},{3,1},{4,2},{5,3},{6,4},{7,5},{8,56},{9,57},{10,... | collective-permute-start | bytes 1880072 | tf_op jit(solution)/shard_map/ppermute | solution.py:29
  22.7 32.8 %collective-permute-start.3 = (bf16[272,1152]{1,0:T(8,128)(2,1)S(1)}, bf16[272,1152]{1,0:T(8,128)(2,1)}, u32[]{:S(2)}, u32[]{:S(2)}) collective-permute-start(bf16[272,1152]{1,0:T(8,128)(2,1)S(1)} %concatenate.48), channel_id=1, source_target_pairs={{0,4},{1,5},{2,6},{3,7},{4,0},{5,1},{6,2},{7,3},{8,40},{9,41},{10,... | collective-permute-start | bytes 1880072 | tf_op jit(solution)/shard_map/ppermute | solution.py:29
  27.6 29.9 %collective-permute-start.5 = (bf16[272,1152]{1,0:T(8,128)(2,1)S(1)}, bf16[272,1152]{1,0:T(8,128)(2,1)S(1)}, u32[]{:S(2)}, u32[]{:S(2)}) collective-permute-start(bf16[272,1152]{1,0:T(8,128)(2,1)S(1)} %concatenate.50), channel_id=1, source_target_pairs={{0,8},{1,9},{2,10},{3,11},{4,12},{5,13},{6,14},{7,15},{8,0},{9,1},... | collective-permute-start | bytes 1880072 | tf_op jit(solution)/shard_map/ppermute | solution.py:29
  42.5 15.4 %collective-permute-start.12 = (bf16[272,1152]{1,0:T(8,128)(2,1)S(1)}, bf16[272,1152]{1,0:T(8,128)(2,1)S(1)}, u32[]{:S(2)}, u32[]{:S(2)}) collective-permute-start(bf16[272,1152]{1,0:T(8,128)(2,1)S(1)} %concatenate.48), channel_id=1, source_target_pairs={{0,8},{1,9},{2,10},{3,11},{4,12},{5,13},{6,14},{7,15},{8,0},{9,1},... | collective-permute-start | bytes 1880072 | tf_op jit(solution)/shard_map/ppermute | solution.py:29
  54.1 8.1 %collective-permute-start.9 = (bf16[272,1152]{1,0:T(8,128)(2,1)S(1)}, bf16[272,1152]{1,0:T(8,128)(2,1)S(1)}, u32[]{:S(2)}, u32[]{:S(2)}) collective-permute-start(bf16[272,1152]{1,0:T(8,128)(2,1)S(1)} %collective-permute-done.8), channel_id=1, source_target_pairs={{0,8},{1,9},{2,10},{3,11},{4,12},{5,13},{6,14},{7,15},{8,0},{9,1},... | collective-permute-start | bytes 1880072 | tf_op jit(solution)/shard_map/ppermute | solution.py:29
  140.7 11.1 %collective-permute-start.16 = (bf16[288,1152]{1,0:T(8,128)(2,1)S(1)}, bf16[288,1152]{1,0:T(8,128)(2,1)S(1)}, u32[]{:S(2)}, u32[]{:S(2)}) collective-permute-start(bf16[288,1152]{1,0:T(8,128)(2,1)S(1)} %get-tuple-element.14), channel_id=1, source_target_pairs={{0,2},{1,3},{2,4},{3,5},{4,6},{5,7},{6,0},{7,1},{8,24},{9,25},{10,... | collective-permute-start | bytes 1990664 | tf_op jit(solution)/shard_map/ppermute | solution.py:29
  142.1 9.8 %collective-permute-start.17 = (bf16[288,1152]{1,0:T(8,128)(2,1)S(1)}, bf16[288,1152]{1,0:T(8,128)(2,1)S(1)}, u32[]{:S(2)}, u32[]{:S(2)}) collective-permute-start(bf16[288,1152]{1,0:T(8,128)(2,1)S(1)} %get-tuple-element.16), channel_id=1, source_target_pairs={{0,6},{1,7},{2,0},{3,1},{4,2},{5,3},{6,4},{7,5},{8,56},{9,57},{10,... | collective-permute-start | bytes 1990664 | tf_op jit(solution)/shard_map/ppermute | solution.py:29
  143.4 15.9 %collective-permute-start.18 = (bf16[288,1152]{1,0:T(8,128)(2,1)S(1)}, bf16[288,1152]{1,0:T(8,128)(2,1)}, u32[]{:S(2)}, u32[]{:S(2)}) collective-permute-start(bf16[288,1152]{1,0:T(8,128)(2,1)S(1)} %get-tuple-element.15), channel_id=1, source_target_pairs={{0,4},{1,5},{2,6},{3,7},{4,0},{5,1},{6,2},{7,3},{8,40},{9,41},{10,... | collective-permute-start | bytes 1990664 | tf_op jit(solution)/shard_map/ppermute | solution.py:29
  162.2 9.4 %collective-permute-start.20 = (f32[72,1152]{1,0:T(8,128)S(1)}, f32[72,1152]{1,0:T(8,128)}, u32[]{:S(2)}, u32[]{:S(2)}) collective-permute-start(f32[72,1152]{1,0:T(8,128)S(1)} %get-tuple-element.19), channel_id=1, source_target_pairs={{0,48},{1,49},{2,50},{3,51},{4,52},{5,53},{6,54},{7,55},{8,14},{9,... | collective-permute-start | bytes 995336 | tf_op jit(solution)/shard_map/ppermute | solution.py:29
  164.0 9.5 %collective-permute-start.21 = (f32[72,1152]{1,0:T(8,128)S(1)}, f32[72,1152]{1,0:T(8,128)}, u32[]{:S(2)}, u32[]{:S(2)}) collective-permute-start(f32[72,1152]{1,0:T(8,128)S(1)} %get-tuple-element.18), channel_id=1, source_target_pairs={{0,32},{1,33},{2,34},{3,35},{4,36},{5,37},{6,38},{7,39},{8,12},{9,... | collective-permute-start | bytes 995336 | tf_op jit(solution)/shard_map/ppermute | solution.py:29
  174.7 10.3 %collective-permute-start.22 = (f32[72,1152]{1,0:T(8,128)S(1)}, f32[72,1152]{1,0:T(8,128)S(1)}, u32[]{:S(2)}, u32[]{:S(2)}) collective-permute-start(f32[72,1152]{1,0:T(8,128)S(1)} %get-tuple-element.5), channel_id=1, source_target_pairs={{0,64},{1,65},{2,66},{3,67},{4,68},{5,69},{6,70},{7,71},{8,72},{9,... | collective-permute-start | bytes 995336 | tf_op jit(solution)/shard_map/ppermute | solution.py:29
  175.1 9.9 %collective-permute-start.23 = (f32[72,1152]{1,0:T(8,128)S(1)}, f32[72,1152]{1,0:T(8,128)S(1)}, u32[]{:S(2)}, u32[]{:S(2)}) collective-permute-start(f32[72,1152]{1,0:T(8,128)S(1)} %get-tuple-element.5), channel_id=1, source_target_pairs={{0,65},{1,64},{2,67},{3,66},{4,69},{5,68},{6,71},{7,70},{8,73},{9,... | collective-permute-start | bytes 995336 | tf_op jit(solution)/shard_map/ppermute | solution.py:29
  177.7 11.6 %collective-permute-start.24 = (f32[72,1152]{1,0:T(8,128)S(1)}, f32[72,1152]{1,0:T(8,128)S(1)}, u32[]{:S(2)}, u32[]{:S(2)}) collective-permute-start(f32[72,1152]{1,0:T(8,128)S(1)} %get-tuple-element.5), channel_id=1, source_target_pairs={{0,1},{1,0},{2,3},{3,2},{4,5},{5,4},{6,7},{7,6},{8,9},{9,8},{10,11... | collective-permute-start | bytes 995336 | tf_op jit(solution)/shard_map/ppermute | solution.py:29
  190.3 9.6 %collective-permute-start.26 = (f32[72,1152]{1,0:T(8,128)S(1)}, f32[72,1152]{1,0:T(8,128)S(1)}, u32[]{:S(2)}, u32[]{:S(2)}) collective-permute-start(f32[72,1152]{1,0:T(8,128)S(1)} %get-tuple-element.3), channel_id=1, source_target_pairs={{0,48},{1,49},{2,50},{3,51},{4,52},{5,53},{6,54},{7,55},{8,14},{9,... | collective-permute-start | bytes 995336 | tf_op jit(solution)/shard_map/ppermute | solution.py:29
  192.2 8.2 %collective-permute-start.27 = (f32[72,1152]{1,0:T(8,128)S(1)}, f32[72,1152]{1,0:T(8,128)S(1)}, u32[]{:S(2)}, u32[]{:S(2)}) collective-permute-start(f32[72,1152]{1,0:T(8,128)S(1)} %get-tuple-element.3), channel_id=1, source_target_pairs={{0,32},{1,33},{2,34},{3,35},{4,36},{5,37},{6,38},{7,39},{8,12},{9,... | collective-permute-start | bytes 995336 | tf_op jit(solution)/shard_map/ppermute | solution.py:29
  200.5 20.1 %collective-permute-start.28 = (f32[288,1152]{1,0:T(8,128)S(1)}, f32[288,1152]{1,0:T(8,128)}, u32[]{:S(2)}, u32[]{:S(2)}) collective-permute-start(f32[288,1152]{1,0:T(8,128)S(1)} %constant_dynamic-update-slice_fusion.8), channel_id=1, source_target_pairs={{0,2},{1,3},{2,4},{3,5},{4,6},{5,7},{6,0},{7,1},{8,24},{9,25},{10,... | collective-permute-start | bytes 3981320 | tf_op jit(solution)/shard_map/ppermute | solution.py:29
  201.2 32.2 %collective-permute-start.29 = (f32[288,1152]{1,0:T(8,128)S(1)}, f32[288,1152]{1,0:T(8,128)}, u32[]{:S(2)}, u32[]{:S(2)}) collective-permute-start(f32[288,1152]{1,0:T(8,128)S(1)} %constant_dynamic-update-slice_fusion.8), channel_id=1, source_target_pairs={{0,6},{1,7},{2,0},{3,1},{4,2},{5,3},{6,4},{7,5},{8,56},{9,57},{10,... | collective-permute-start | bytes 3981320 | tf_op jit(solution)/shard_map/ppermute | solution.py:29
  203.3 31.6 %collective-permute-start.30 = (f32[288,1152]{1,0:T(8,128)S(1)}, f32[288,1152]{1,0:T(8,128)S(1)}, u32[]{:S(2)}, u32[]{:S(2)}) collective-permute-start(f32[288,1152]{1,0:T(8,128)S(1)} %constant_dynamic-update-slice_fusion.8), channel_id=1, source_target_pairs={{0,4},{1,5},{2,6},{3,7},{4,0},{5,1},{6,2},{7,3},{8,40},{9,41},{10,... | collective-permute-start | bytes 3981320 | tf_op jit(solution)/shard_map/ppermute | solution.py:29
  234.9 17.6 %collective-permute-start.31 = (f32[1152,1152]{1,0:T(8,128)S(1)}, f32[1152,1152]{1,0:T(8,128)S(1)}, u32[]{:S(2)}, u32[]{:S(2)}) collective-permute-start(f32[1152,1152]{1,0:T(8,128)S(1)} %constant_dynamic-update-slice_fusion.4), channel_id=1, source_target_pairs={{0,8},{1,9},{2,10},{3,11},{4,12},{5,13},{6,14},{7,15},{8,0},{9,1},... | collective-permute-start | bytes 15925256 | tf_op jit(solution)/shard_map/ppermute | solution.py:29
  (20 other events, 151.4 us)

commit v2 on v1

v2 whole, which is shorter than its diff:
```python
import math

import jax
import jax.numpy as jnp
from jax import lax
from jax.experimental import pallas as pl
from jax.experimental.pallas import tpu as pltpu
from jax.sharding import Mesh, PartitionSpec as P

AXES = ("zl", "y", "c", "x", "zh")
SIZES = (2, 4, 2, 4, 2)
BF16 = jnp.bfloat16
F32 = jnp.float32
WIDE = 1152
ROWS = 2048
VMEM_BYTES = 58 * 1024 * 1024


def routes(move):
    pairs = []
    index = 0
    for zl in range(2):
        for y in range(4):
            for c in range(2):
                for x in range(4):
                    for zh in range(2):
                        tzl, ty, tc, tx, tzh = move(zl, y, c, x, zh)
                        pairs.append((index, (((tzl * 4 + ty) * 2 + tc) * 4 + tx) * 2 + tzh))
                        index += 1
    return pairs


def send(value, move):
    return lax.ppermute(value, AXES, routes(move))


def other_core(zl, y, c, x, zh):
    return (zl, y, 1 - c, x, zh)


def z_pair(swap):
    def move(zl, y, c, x, zh):
        return (1 - zl, y, c, x, zh if (c ^ swap) == 0 else 1 - zh)

    return move


def ring(by, swap):
    def move(zl, y, c, x, zh):
        if (c ^ swap) == 0:
            return (zl, y, c, (x + by) % 4, zh)
        return (zl, (y + by) % 4, c, x, zh)

    return move


def z_ring(by):
    def move(zl, y, c, x, zh):
        z = (zh * 2 + zl + by) % 4
        return (z % 2, y, c, x, z // 2)

    return move


def with_partner(value, swap):
    got = send(value, z_pair(swap))
    return jnp.concatenate([value[:128], got[:128], value[128:129], got[128:129], value[130:144]], axis=0)


def rows_of_ids(block_ref):
    coded = block_ref[256:272, :256].astype(F32)
    parts = [coded[i : i + 1, :128] * 64.0 + coded[i : i + 1, 128:] for i in range(2)]
    return jnp.broadcast_to(jnp.concatenate(parts, axis=1), (8, 256))


def project_kernel(*refs):
    own, over, own_far, over_far, head_mine, head_theirs = refs[:6]
    proj, unit, rows, ids_mine, ids_theirs = refs[-5:]
    for part, (near, far) in enumerate(((own, own_far), (over, over_far))):
        at = pl.ds(part * 256, 256)
        block = near[:256, :]
        rows[at, :] = block
        proj[at, :] = jnp.dot(block, head_mine[...], preferred_element_type=F32)
        other = jnp.dot(far[:256, :], head_theirs[...], preferred_element_type=F32)
        length = jnp.sqrt(jnp.sum(other * other, axis=1, keepdims=True) + 1e-06)
        unit[at, :] = (other / length).astype(BF16)
        ids_mine[part * 8 : part * 8 + 8, :] = rows_of_ids(near)
        ids_theirs[part * 8 : part * 8 + 8, :] = rows_of_ids(far)


def project(turn, blocks, heads, held):
    whole = pl.BlockSpec(memory_space=pltpu.VMEM)
    shapes = [
        jax.ShapeDtypeStruct((ROWS, WIDE), F32),
        jax.ShapeDtypeStruct((ROWS, WIDE), BF16),
        jax.ShapeDtypeStruct((ROWS, WIDE), BF16),
        jax.ShapeDtypeStruct((64, 256), F32),
        jax.ShapeDtypeStruct((64, 256), F32),
    ]
    return pl.pallas_call(
        project_kernel,
        grid=(1,),
        out_shape=shapes,
        in_specs=[whole] * 6 + [pl.BlockSpec(memory_space=pl.ANY)] * len(held),
        out_specs=[pl.BlockSpec((512, WIDE), lambda i: (turn, 0))] * 3
        + [pl.BlockSpec((16, 256), lambda i: (turn, 0))] * 2,
        input_output_aliases={6 + i: i for i in range(len(held))},
        compiler_params=pltpu.CompilerParams(vmem_limit_bytes=40 * 1024 * 1024),
        cost_estimate=pl.CostEstimate(
            flops=2 * 1024 * WIDE * WIDE, bytes_accessed=12_000_000, transcendentals=0
        ),
        name="project",
    )(*blocks, *heads, *held)


def pair_kernel(
    at_ref, knob_ref, proj, rows, ids_mine, unit, ids_theirs, own, one, three, two, total, coef
):
    step = pl.program_id(0)
    half_scale, half_bias, half = knob_ref[0], knob_ref[1], knob_ref[2]
    projected = proj[...]
    length = jnp.sqrt(jnp.sum(projected * projected, axis=1, keepdims=True) + 1e-06)
    near = (projected / length).astype(BF16)
    eye = lax.broadcasted_iota(jnp.int32, (256, 256), 0) == lax.broadcasted_iota(
        jnp.int32, (256, 256), 1
    )
    columns = [
        jnp.sum(jnp.where(eye, ids_mine[i * 8 : i * 8 + 1, :], 0.0), axis=1, keepdims=True)
        for i in range(2)
    ]
    column = jnp.concatenate(columns, axis=0)
    for part in range(8):
        at = pl.ds(part * 256, 256)
        cosine = lax.dot_general(
            near, unit[at, :], (((1,), (1,)), ((), ())), preferred_element_type=F32
        )
        base = jnp.where(column == ids_theirs[part * 8 : part * 8 + 1, :], -half, half)
        coef[:, at] = (jnp.tanh(cosine * half_scale + half_bias) * half + base).astype(BF16)
    grad = jnp.dot(coef[...], unit[...], preferred_element_type=F32)
    direction = proj[...] / length
    radial = jnp.sum(grad * direction, axis=1, keepdims=True)
    back = ((grad - radial * direction) / length).astype(BF16)
    part = lax.dot_general(
        rows[...], back, (((0,), (0,)), ((), ())), preferred_element_type=F32
    )

    @pl.when(step == 0)
    def _():
        total[...] = part

    @pl.when(step > 0)
    def _():
        total[...] += part

    @pl.when(step == 3)
    def _():
        for by, out in ((0, own), (1, one), (3, three), (2, two)):
            place = pl.multiple_of(lax.rem(at_ref[0] + by, 4) * 288, 288)
            out[...] = total[pl.ds(place, 288), :].astype(out.dtype)


def pair_tile(at, knobs, held):
    proj, unit, rows, ids_mine, ids_theirs = held
    fixed = lambda i: (0, 0)
    moving = lambda i: (i, 0)
    smem = pl.BlockSpec(memory_space=pltpu.SMEM)
    return pl.pallas_call(
        pair_kernel,
        grid=(4,),
        out_shape=[jax.ShapeDtypeStruct((288, WIDE), kind) for kind in (F32, BF16, BF16, BF16)],
        in_specs=[
            smem,
            smem,
            pl.BlockSpec((512, WIDE), moving),
            pl.BlockSpec((512, WIDE), moving),
            pl.BlockSpec((16, 256), moving),
            pl.BlockSpec((ROWS, WIDE), fixed, pipeline_mode=pl.Buffered(1)),
            pl.BlockSpec((64, 256), fixed),
        ],
        out_specs=[pl.BlockSpec((288, WIDE), fixed)] * 4,
        scratch_shapes=[pltpu.VMEM((WIDE, WIDE), F32), pltpu.VMEM((512, ROWS), BF16)],
        compiler_params=pltpu.CompilerParams(
            dimension_semantics=("arbitrary",), vmem_limit_bytes=VMEM_BYTES
        ),
        cost_estimate=pl.CostEstimate(
            flops=2 * ROWS * WIDE * (2 * ROWS + WIDE),
            bytes_accessed=24_000_000,
            transcendentals=ROWS * ROWS,
        ),
        name="pair_tile",
    )(at, knobs, proj, rows, ids_mine, unit, ids_theirs)


def place_kernel(where_ref, *refs):
    pieces, outs = refs[:8], refs[8:10]
    narrow, wide, in_sems, out_sems = refs[10:]
    loads = [
        pltpu.make_async_copy(piece, narrow.at[i], in_sems.at[i]) for i, piece in enumerate(pieces)
    ]
    for load in loads:
        load.start()

    def stores(i):
        head = where_ref[0] if i < 4 else 1 - where_ref[0]
        row = pl.multiple_of(where_ref[1 + i] * 288, 288)
        for h in range(2):
            copy = pltpu.make_async_copy(
                wide.at[i], outs[h].at[pl.ds(row, 288), :], out_sems.at[i]
            )
            yield head == h, copy

    for i in range(8):
        loads[i].wait()
        wide[i] = narrow[i].astype(F32)
        for here, copy in stores(i):
            pl.when(here)(copy.start)
    for i in range(8):
        for here, copy in stores(i):
            pl.when(here)(copy.wait)


def place(where, pieces):
    return pl.pallas_call(
        place_kernel,
        out_shape=[jax.ShapeDtypeStruct((WIDE, WIDE), F32)] * 2,
        in_specs=[pl.BlockSpec(memory_space=pltpu.SMEM)]
        + [pl.BlockSpec(memory_space=pl.ANY)] * 8,
        out_specs=[pl.BlockSpec(memory_space=pl.ANY)] * 2,
        scratch_shapes=[
            pltpu.VMEM((8, 288, WIDE), BF16),
            pltpu.VMEM((8, 288, WIDE), F32),
            pltpu.SemaphoreType.DMA((8,)),
            pltpu.SemaphoreType.DMA((8,)),
        ],
        compiler_params=pltpu.CompilerParams(vmem_limit_bytes=VMEM_BYTES),
        name="place",
    )(where, *pieces)


def added(total, parts):
    for part in parts:
        total = total + part.astype(F32)
    return total


def scattered(value, by_route, mine):
    rows = value.shape[0] // 4
    total = lax.dynamic_slice_in_dim(value, mine * rows, rows, 0)
    parts = []
    for by in (1, 3, 2):
        part = lax.dynamic_slice_in_dim(value, lax.rem(mine + by, 4) * rows, rows, 0)
        parts.append(send(part, by_route(by)))
    return added(total, parts)


def local(image_embed, text_embed, image_head, text_head, pair_ids, logit_scale, logit_bias):
    first = lax.axis_index("c") == 0
    scale = logit_scale[0]
    half = scale * (0.5 / math.sqrt(16384))
    knobs = jnp.stack([scale * 0.5, logit_bias[0] * 0.5, half])

    ids_row = jnp.concatenate(
        [(pair_ids // 64).astype(BF16), (pair_ids % 64).astype(BF16), jnp.zeros((896,), BF16)]
    )[None]
    ids_rows = jnp.concatenate([ids_row, jnp.zeros((15, WIDE), BF16)], axis=0)
    mine = jnp.concatenate([jnp.where(first, image_embed, text_embed), ids_rows], axis=0)
    theirs = jnp.concatenate([jnp.where(first, text_embed, image_embed), ids_rows], axis=0)
    heads = (jnp.where(first, image_head, text_head), jnp.where(first, text_head, image_head))

    mine = with_partner(mine, 0)
    theirs = with_partner(theirs, 1)
    held = ()
    for turn, by in enumerate((0, 1, 3, 2)):
        own = mine if by == 0 else send(mine, ring(by, 0))
        own_far = theirs if by == 0 else send(theirs, ring(by, 1))
        over, over_far = send(own_far, other_core), send(own, other_core)
        held = project(turn, (own, over, own_far, over_far), heads, held)

    at_x = lax.axis_index("x")
    at_y = lax.axis_index("y")
    at_first = jnp.where(first, at_x, at_y)
    at_second = jnp.where(first, at_y, at_x)
    part, *away = pair_tile(at_first[None], knobs, held)
    part = added(part, [send(piece, ring(by, 0)) for by, piece in zip((1, 3, 2), away)])
    part = scattered(part, lambda by: ring(by, 1), at_second)
    moved = [send(part, z_ring(by)) for by in (1, 3, 2)]
    at_z = lax.axis_index("zh") * 2 + lax.axis_index("zl")
    stack = jnp.zeros((4,) + part.shape, F32)
    for by, piece in zip((0, 1, 3, 2), [part] + moved):
        stack = lax.dynamic_update_slice_in_dim(stack, piece[None], lax.rem(at_z + 4 - by, 4), 0)
    part = ((stack[0] + stack[1]) + (stack[2] + stack[3])).astype(BF16)

    quarter = jnp.zeros((288, WIDE), BF16)
    for by in (0, 1, 3, 2):
        piece = part if by == 0 else send(part, ring(by, 1))
        quarter = lax.dynamic_update_slice_in_dim(
            quarter, piece, lax.rem(at_second + 4 - by, 4) * 72, 0
        )
    pieces = [quarter] + [send(quarter, ring(by, 0)) for by in (1, 3, 2)]
    pieces = pieces + [send(piece, other_core) for piece in pieces]
    where = [lax.axis_index("c")]
    for at in (at_first, at_second):
        where += [lax.rem(at + 4 - by, 4) for by in (0, 1, 3, 2)]
    return tuple(place(jnp.stack(where).astype(jnp.int32), pieces))


def solution(mesh):
    split = Mesh(mesh.devices.reshape(SIZES), AXES)
    every = P(AXES)
    return jax.shard_map(
        local,
        mesh=split,
        in_specs=(every, every, P(), P(), every, P(), P()),
        out_specs=(P(), P()),
        check_vma=False,
    )
```

time: 258 us -> 226 us (0.88)
  Pallas kernels: 0 us -> 70.4 us
  matrix products: 69.7 us -> 0 us
  waiting for transfers between devices: 80.7 us -> 55.2 us
  local copies, waits for them, and re-layouts: 28.6 us -> 13 us
  starting transfers between devices: 65.1 us -> 73.8 us
    pallas_call x0 -> x6, Pallas kernels: none -> 70.4 us  [the longest x1 42.3 us: pair_tile(): pl.pallas_call(pair_kernel, grid=(4,), out_shape=[jax.ShapeDtypeStruct((2...]
    dot_general x4 -> x0, matrix products: 69.7 us -> none  [the longest x1 37.1 us: local(): grad = jnp.dot(coef, unit_theirs, preferred_element_type=F32)]
    ppermute x32 -> x35, waiting for transfers between devices: 80.7 us -> 55.2 us  [send(): return lax.ppermute(value, AXES, routes(move))]
    ppermute x32 -> x35, starting transfers between devices: 65.1 us -> 73.8 us  [send(): return lax.ppermute(value, AXES, routes(move))]
    unnamed x37 -> x38, local copies, waits for them, and re-layouts: 16.1 us -> 10.8 us
    dynamic_update_slice x7 -> x3, local copies, waits for them, and re-layouts: 3.08 us -> 0.06 us  [local(): lax.dynamic_update_slice_in_dim(quarter, piece, lax.rem(at_second + 4 - b...]
    slice x14 -> x0, local copies, waits for them, and re-layouts: 2.77 us -> none  [block_ids(): block[256:258, :256].astype(F32)]
    select_n x1 -> x2, other arithmetic: 4.81 us -> 6.51 us  [the longest x1 5.4 us: local(): jnp.where(first, text_head, image_head)]
  transfers between devices with their start and end apart: 32 -> 35, of which waited for: 16 -> 18; matrix products, arithmetic and copies ran while one was open for 8% -> 3% of each run, Pallas kernels for 0% -> 7%
where the time goes in v2:
time: 226 us
  starting transfers between devices  73.8 us (33%)
  Pallas kernels  70.4 us (31%)
  waiting for transfers between devices  55.2 us (24%)
  local copies, waits for them, and re-layouts  13 us (6%)
  other arithmetic  10.8 us (5%)
  between operations  2.41 us (1%)
    ppermute x35, starting transfers between devices, send(): return lax.ppermute(value, AXES, routes(move))  73.8 us
    ppermute x35, waiting for transfers between devices, send(): return lax.ppermute(value, AXES, routes(move))  55.2 us
    pallas_call x1, Pallas kernels, pair_tile(): pl.pallas_call(pair_kernel, grid=(4,), out_shape=[jax.ShapeDtypeStruct((2...  42.3 us
    pallas_call x4, Pallas kernels, project(): pl.pallas_call(project_kernel, grid=(1,), out_shape=shapes, in_specs=[who...  22.1 us
    unnamed x38, local copies, waits for them, and re-layouts  10.8 us
    pallas_call x1, Pallas kernels, place(): pl.pallas_call(place_kernel, out_shape=[jax.ShapeDtypeStruct((WIDE, WIDE)...  5.99 us
    select_n x1, other arithmetic, local(): jnp.where(first, text_head, image_head)  5.4 us
  transfers between devices with their start and end apart: 35, of which 18 were waited for; matrix products, arithmetic and copies ran while one was open for 3% of the time, Pallas kernels for 7%

profile of v2, /device:TPU:1, one launch (start us, length us, event | category | flops | bytes accessed | tf_op | source)
XLA Modules:
  0.0 225.7 jit_solution(15782076107099324584)
XLA Ops:
  7.5 2.6 %collective-permute-done.2 = bf16[144,1152]{1,0:T(8,128)(2,1)S(1)} collective-permute-done((bf16[144,1152]{1,0:T(8,128)(2,1)S(1)}, bf16[144,1152]{1,0:T(8,128)(2,1)S(1)}, u32[]{:S(2)}, u32[]{:S(2)}) %collective-permute-start.2) | collective-permute-done | bytes 331808 | tf_op jit(solution)/shard_map/ppermute | solution.py:34
  10.6 6.7 %collective-permute-start.14 = (bf16[272,1152]{1,0:T(8,128)(2,1)S(1)}, bf16[272,1152]{1,0:T(8,128)(2,1)S(1)}, u32[]{:S(2)}, u32[]{:S(2)}) collective-permute-start(bf16[272,1152]{1,0:T(8,128)(2,1)S(1)} %concatenate.22.refs_2_), channel_id=1, source_target_pairs={{0,8},{1,9},{2,10},{3,11},{4,12},{5,13},{6,14},{7,15},{8,0},{9,1},... | collective-permute-start | bytes 1880072 | tf_op jit(solution)/shard_map/ppermute | solution.py:34
  25.9 7.1 %collective-permute-done.11.refs_2_ = bf16[272,1152]{1,0:T(8,128)(2,1)S(1)} collective-permute-done((bf16[272,1152]{1,0:T(8,128)(2,1)S(1)}, bf16[272,1152]{1,0:T(8,128)(2,1)S(1)}, u32[]{:S(2)}, u32[]{:S(2)}) %collective-permute-start.11) | collective-permute-done | bytes 626720 | tf_op jit(solution)/shard_map/ppermute | solution.py:34
  33.0 3.2 %collective-permute-start.1 = (bf16[272,1152]{1,0:T(8,128)(2,1)S(1)}, bf16[272,1152]{1,0:T(8,128)(2,1)}, u32[]{:S(2)}, u32[]{:S(2)}) collective-permute-start(bf16[272,1152]{1,0:T(8,128)(2,1)S(1)} %concatenate.20.refs_0_), channel_id=1, source_target_pairs={{0,4},{1,5},{2,6},{3,7},{4,0},{5,1},{6,2},{7,3},{8,40},{9,41},{10,... | collective-permute-start | bytes 1880072 | tf_op jit(solution)/shard_map/ppermute | solution.py:34
  36.4 3.2 %collective-permute-start.12 = (bf16[272,1152]{1,0:T(8,128)(2,1)S(1)}, bf16[272,1152]{1,0:T(8,128)(2,1)S(1)}, u32[]{:S(2)}, u32[]{:S(2)}) collective-permute-start(bf16[272,1152]{1,0:T(8,128)(2,1)S(1)} %collective-permute-done.11.refs_2_), channel_id=1, source_target_pairs={{0,8},{1,9},{2,10},{3,11},{4,12},{5,13},{6,14},{7,15},{8,0},{9,1},... | collective-permute-start | bytes 1880072 | tf_op jit(solution)/shard_map/ppermute | solution.py:34
  39.7 10.1 %collective-permute-start.8 = (bf16[272,1152]{1,0:T(8,128)(2,1)}, bf16[272,1152]{1,0:T(8,128)(2,1)}, u32[]{:S(2)}, u32[]{:S(2)}) collective-permute-start(bf16[272,1152]{1,0:T(8,128)(2,1)} %collective-permute-done.7.refs_2_), channel_id=1, source_target_pairs={{0,8},{1,9},{2,10},{3,11},{4,12},{5,13},{6,14},{7,15},{8,0},{9,1},... | collective-permute-start | bytes 1880072 | tf_op jit(solution)/shard_map/ppermute | solution.py:34
  51.1 5.4 %broadcast_select_fusion = (bf16[1152,1152]{1,0:T(8,128)(2,1)}, bf16[1152,1152]{1,0:T(8,128)(2,1)}) fusion(bf16[1152,1152]{1,0:T(8,128)(2,1)} %param.10, bf16[1152,1152]{1,0:T(8,128)(2,1)} %param.9, pred[]{:T(512)S(6)} %eq.5), kind=kLoop, calls=%fused_computation | loop fusion | flops 2654208 | bytes 10616833 | tf_op jit(solution)/shard_map/jit(_where)/select_n | solution.py:268
  65.5 4.6 %project.4 = (f32[2048,1152]{1,0:T(8,128)}, bf16[2048,1152]{1,0:T(8,128)(2,1)S(1)}, bf16[2048,1152]{1,0:T(8,128)(2,1)}, f32[64,256]{1,0:T(8,128)S(1)}, f32[64,256]{1,0:T(8,128)S(1)}) custom-call(bf16[272,1152]{1,0:T(8,128)(2,1)S(1)} %concatenate.20.refs_0_, bf16[272,1152]{1,0:T(8,128)(2,1)S(1)} %copy-done.10, bf16[272,1152]{1,0:T(8,128)(2,1)S(1)} %concatenate.22.refs_2_, ...), custom_call_target="tpu_custom_call" | custom-call | flops 2717908992 | bytes 12000000 | tf_op jit(solution)/shard_map/project/pallas_call | solution.py:100
  70.1 5.8 %project.5 = (f32[2048,1152]{1,0:T(8,128)}, bf16[2048,1152]{1,0:T(8,128)(2,1)S(1)}, bf16[2048,1152]{1,0:T(8,128)(2,1)}, f32[64,256]{1,0:T(8,128)S(1)}, f32[64,256]{1,0:T(8,128)S(1)}) custom-call(bf16[272,1152]{1,0:T(8,128)(2,1)} %collective-permute-done.10.refs_0_, ...), custom_call_target="tpu_custom_call", output_to_operand_aliasing={{0}: (6, {}), {1}: (7, {}), {2}: (8, {}), {3}: (9, {}), {4}... | custom-call | flops 2717908992 | bytes 12000000 | tf_op jit(solution)/shard_map/project/pallas_call | solution.py:100
  75.9 6.1 %project.6 = (f32[2048,1152]{1,0:T(8,128)}, bf16[2048,1152]{1,0:T(8,128)(2,1)S(1)}, bf16[2048,1152]{1,0:T(8,128)(2,1)}, f32[64,256]{1,0:T(8,128)S(1)}, f32[64,256]{1,0:T(8,128)S(1)}) custom-call(bf16[272,1152]{1,0:T(8,128)(2,1)} %collective-permute-done.6.refs_0_, ...), custom_call_target="tpu_custom_call", output_to_operand_aliasing={{0}: (6, {}), {1}: (7, {}), {2}: (8, {}), {3}: (9, {}), {4}... | custom-call | flops 2717908992 | bytes 12000000 | tf_op jit(solution)/shard_map/project/pallas_call | solution.py:100
  82.0 5.6 %project.7 = (f32[2048,1152]{1,0:T(8,128)}, bf16[2048,1152]{1,0:T(8,128)(2,1)S(1)}, bf16[2048,1152]{1,0:T(8,128)(2,1)}, f32[64,256]{1,0:T(8,128)S(1)}, f32[64,256]{1,0:T(8,128)S(1)}) custom-call(bf16[272,1152]{1,0:T(8,128)(2,1)} %collective-permute-done.1.refs_0_, ...), custom_call_target="tpu_custom_call", output_to_operand_aliasing={{0}: (6, {}), {1}: (7, {}), {2}: (8, {}), {3}: (9, {}), {4}... | custom-call | flops 2717908992 | bytes 12000000 | tf_op jit(solution)/shard_map/project/pallas_call | solution.py:100
  91.0 42.3 %pair_tile.1 = (f32[288,1152]{1,0:T(8,128)}, bf16[288,1152]{1,0:T(8,128)(2,1)}, bf16[288,1152]{1,0:T(8,128)(2,1)}, bf16[288,1152]{1,0:T(8,128)(2,1)}) custom-call(s32[1]{0:T(128)} %bitcast.9.at_ref, f32[3]{0:T(128)} %pad_maximum_fusion.3.knob_ref, f32[2048,1152]{1,0:T(8,128)} %get-tuple-element.41.proj, bf16[2048,1152]{1,0:T(8,128)(2,1)} %get-tuple-element.42.rows, ...), custom_call_target="tpu_custom_call" | custom-call | flops 24763170816 | bytes 24000000 | tf_op jit(solution)/shard_map/pair_tile/pallas_call | solution.py:167
  137.9 7.2 %collective-permute-done.16 = bf16[288,1152]{1,0:T(8,128)(2,1)S(1)} collective-permute-done((bf16[288,1152]{1,0:T(8,128)(2,1)}, bf16[288,1152]{1,0:T(8,128)(2,1)S(1)}, u32[]{:S(2)}, u32[]{:S(2)}) %collective-permute-start.16) | collective-permute-done | bytes 663584 | tf_op jit(solution)/shard_map/ppermute | solution.py:34
  145.4 8.0 %collective-permute-done.18 = bf16[288,1152]{1,0:T(8,128)(2,1)S(1)} collective-permute-done((bf16[288,1152]{1,0:T(8,128)(2,1)}, bf16[288,1152]{1,0:T(8,128)(2,1)S(1)}, u32[]{:S(2)}, u32[]{:S(2)}) %collective-permute-start.18) | collective-permute-done | bytes 663584 | tf_op jit(solution)/shard_map/ppermute | solution.py:34
  159.7 2.9 %collective-permute-done.19 = f32[72,1152]{1,0:T(8,128)S(1)} collective-permute-done((f32[72,1152]{1,0:T(8,128)S(1)}, f32[72,1152]{1,0:T(8,128)S(1)}, u32[]{:S(2)}, u32[]{:S(2)}) %collective-permute-start.19) | collective-permute-done | bytes 331808 | tf_op jit(solution)/shard_map/ppermute | solution.py:34
  163.0 3.7 %collective-permute-done.21 = f32[72,1152]{1,0:T(8,128)} collective-permute-done((f32[72,1152]{1,0:T(8,128)S(1)}, f32[72,1152]{1,0:T(8,128)}, u32[]{:S(2)}, u32[]{:S(2)}) %collective-permute-start.21) | collective-permute-done | bytes 331808 | tf_op jit(solution)/shard_map/ppermute | solution.py:34
  168.1 2.6 %collective-permute-start.23 = (f32[72,1152]{1,0:T(8,128)S(1)}, f32[72,1152]{1,0:T(8,128)S(1)}, u32[]{:S(2)}, u32[]{:S(2)}) collective-permute-start(f32[72,1152]{1,0:T(8,128)S(1)} %get-tuple-element.53), channel_id=1, source_target_pairs={{0,65},{1,64},{2,67},{3,66},{4,69},{5,68},{6,71},{7,70},{8,73},{9,... | collective-permute-start | bytes 995336 | tf_op jit(solution)/shard_map/ppermute | solution.py:34
  171.5 4.8 %collective-permute-done.22 = f32[72,1152]{1,0:T(8,128)S(1)} collective-permute-done((f32[72,1152]{1,0:T(8,128)S(1)}, f32[72,1152]{1,0:T(8,128)S(1)}, u32[]{:S(2)}, u32[]{:S(2)}) %collective-permute-start.22) | collective-permute-done | bytes 331808 | tf_op jit(solution)/shard_map/ppermute | solution.py:34
  176.4 7.8 %collective-permute-done.24 = f32[72,1152]{1,0:T(8,128)S(1)} collective-permute-done((f32[72,1152]{1,0:T(8,128)S(1)}, f32[72,1152]{1,0:T(8,128)S(1)}, u32[]{:S(2)}, u32[]{:S(2)}) %collective-permute-start.24) | collective-permute-done | bytes 331808 | tf_op jit(solution)/shard_map/ppermute | solution.py:34
  193.1 2.9 %collective-permute-start.29 = (bf16[288,1152]{1,0:T(8,128)(2,1)S(1)}, bf16[288,1152]{1,0:T(8,128)(2,1)S(1)}, u32[]{:S(2)}, u32[]{:S(2)}) collective-permute-start(bf16[288,1152]{1,0:T(8,128)(2,1)S(1)} %constant_dynamic-update-slice_fusion.refs_0_), channel_id=1, source_target_pairs={{0,6},{1,7},{2,0},{3,1},{4,2},{5,3},{6,4},{7,5},{8,56},{9,57},{10,... | collective-permute-start | bytes 1990664 | tf_op jit(solution)/shard_map/ppermute | solution.py:34
  197.1 5.0 %collective-permute-start.31 = (bf16[288,1152]{1,0:T(8,128)(2,1)S(1)}, bf16[288,1152]{1,0:T(8,128)(2,1)S(1)}, u32[]{:S(2)}, u32[]{:S(2)}) collective-permute-start(bf16[288,1152]{1,0:T(8,128)(2,1)S(1)} %constant_dynamic-update-slice_fusion.refs_0_), channel_id=1, source_target_pairs={{0,8},{1,9},{2,10},{3,11},{4,12},{5,13},{6,14},{7,15},{8,0},{9,1},... | collective-permute-start | bytes 1990664 | tf_op jit(solution)/shard_map/ppermute | solution.py:34
  204.4 5.3 %collective-permute-start.32 = (bf16[288,1152]{1,0:T(8,128)(2,1)S(1)}, bf16[288,1152]{1,0:T(8,128)(2,1)}, u32[]{:S(2)}, u32[]{:S(2)}) collective-permute-start(bf16[288,1152]{1,0:T(8,128)(2,1)S(1)} %collective-permute-done.28.refs_1_), channel_id=1, source_target_pairs={{0,8},{1,9},{2,10},{3,11},{4,12},{5,13},{6,14},{7,15},{8,0},{9,1},... | collective-permute-start | bytes 1990664 | tf_op jit(solution)/shard_map/ppermute | solution.py:34
  212.6 5.0 %collective-permute-start.34 = (bf16[288,1152]{1,0:T(8,128)(2,1)S(1)}, bf16[288,1152]{1,0:T(8,128)(2,1)}, u32[]{:S(2)}, u32[]{:S(2)}) collective-permute-start(bf16[288,1152]{1,0:T(8,128)(2,1)S(1)} %collective-permute-done.30.refs_3_), channel_id=1, source_target_pairs={{0,8},{1,9},{2,10},{3,11},{4,12},{5,13},{6,14},{7,15},{8,0},{9,1},... | collective-permute-start | bytes 1990664 | tf_op jit(solution)/shard_map/ppermute | solution.py:34
  219.5 6.0 %place.1 = (f32[1152,1152]{1,0:T(8,128)}, f32[1152,1152]{1,0:T(8,128)}) custom-call(s32[9]{0:T(128)} %stack.45.where_ref, bf16[288,1152]{1,0:T(8,128)(2,1)} %copy-done.13, bf16[288,1152]{1,0:T(8,128)(2,1)} %copy-done.14, bf16[288,1152]{1,0:T(8,128)(2,1)} %copy-done.15, bf16[288,1152]{1,0:T(8,128)(2,1)} %copy-done.16, bf16[288,1152]{1,0:T(8,128)(2,1)} %copy-done.17, ...), custom_call_target="tpu_custom_call" | custom-call | tf_op jit(solution)/shard_map/place/pallas_call | solution.py:223
  (120 shorter events, 59.1 us)
Async XLA Ops:
  5.3 12.1 %collective-permute-start = (bf16[144,1152]{1,0:T(8,128)(2,1)S(1)}, bf16[144,1152]{1,0:T(8,128)(2,1)S(1)}, u32[]{:S(2)}, u32[]{:S(2)}) collective-permute-start(bf16[144,1152]{1,0:T(8,128)(2,1)S(1)} %get-tuple-element.62), channel_id=1, source_target_pairs={{0,64},{1,65},{2,66},{3,67},{4,68},{5,69},{6,70},{7,71},{8,73},{9,... | collective-permute-start | bytes 995336 | tf_op jit(solution)/shard_map/ppermute | solution.py:34
  10.6 11.4 %collective-permute-start.14 = (bf16[272,1152]{1,0:T(8,128)(2,1)S(1)}, bf16[272,1152]{1,0:T(8,128)(2,1)S(1)}, u32[]{:S(2)}, u32[]{:S(2)}) collective-permute-start(bf16[272,1152]{1,0:T(8,128)(2,1)S(1)} %concatenate.22.refs_2_), channel_id=1, source_target_pairs={{0,8},{1,9},{2,10},{3,11},{4,12},{5,13},{6,14},{7,15},{8,0},{9,1},... | collective-permute-start | bytes 1880072 | tf_op jit(solution)/shard_map/ppermute | solution.py:34
  18.0 15.0 %collective-permute-start.11 = (bf16[272,1152]{1,0:T(8,128)(2,1)S(1)}, bf16[272,1152]{1,0:T(8,128)(2,1)S(1)}, u32[]{:S(2)}, u32[]{:S(2)}) collective-permute-start(bf16[272,1152]{1,0:T(8,128)(2,1)S(1)} %concatenate.22.refs_2_), channel_id=1, source_target_pairs={{0,16},{1,17},{2,18},{3,19},{4,20},{5,21},{6,22},{7,23},{8,10},{9,... | collective-permute-start | bytes 1880072 | tf_op jit(solution)/shard_map/ppermute | solution.py:34
  19.3 17.1 %collective-permute-start.10 = (bf16[272,1152]{1,0:T(8,128)(2,1)S(1)}, bf16[272,1152]{1,0:T(8,128)(2,1)}, u32[]{:S(2)}, u32[]{:S(2)}) collective-permute-start(bf16[272,1152]{1,0:T(8,128)(2,1)S(1)} %concatenate.20.refs_0_), channel_id=1, source_target_pairs={{0,2},{1,3},{2,4},{3,5},{4,6},{5,7},{6,0},{7,1},{8,24},{9,25},{10,... | collective-permute-start | bytes 1880072 | tf_op jit(solution)/shard_map/ppermute | solution.py:34
  20.6 19.1 %collective-permute-start.7 = (bf16[272,1152]{1,0:T(8,128)(2,1)S(1)}, bf16[272,1152]{1,0:T(8,128)(2,1)}, u32[]{:S(2)}, u32[]{:S(2)}) collective-permute-start(bf16[272,1152]{1,0:T(8,128)(2,1)S(1)} %concatenate.22.refs_2_), channel_id=1, source_target_pairs={{0,48},{1,49},{2,50},{3,51},{4,52},{5,53},{6,54},{7,55},{8,14},{9,... | collective-permute-start | bytes 1880072 | tf_op jit(solution)/shard_map/ppermute | solution.py:34
  22.9 16.8 %collective-permute-start.6 = (bf16[272,1152]{1,0:T(8,128)(2,1)S(1)}, bf16[272,1152]{1,0:T(8,128)(2,1)}, u32[]{:S(2)}, u32[]{:S(2)}) collective-permute-start(bf16[272,1152]{1,0:T(8,128)(2,1)S(1)} %concatenate.20.refs_0_), channel_id=1, source_target_pairs={{0,6},{1,7},{2,0},{3,1},{4,2},{5,3},{6,4},{7,5},{8,56},{9,57},{10,... | collective-permute-start | bytes 1880072 | tf_op jit(solution)/shard_map/ppermute | solution.py:34
  24.3 25.5 %collective-permute-start.3 = (bf16[272,1152]{1,0:T(8,128)(2,1)S(1)}, bf16[272,1152]{1,0:T(8,128)(2,1)}, u32[]{:S(2)}, u32[]{:S(2)}) collective-permute-start(bf16[272,1152]{1,0:T(8,128)(2,1)S(1)} %concatenate.22.refs_2_), channel_id=1, source_target_pairs={{0,32},{1,33},{2,34},{3,35},{4,36},{5,37},{6,38},{7,39},{8,12},{9,... | collective-permute-start | bytes 1880072 | tf_op jit(solution)/shard_map/ppermute | solution.py:34
  33.0 25.5 %collective-permute-start.1 = (bf16[272,1152]{1,0:T(8,128)(2,1)S(1)}, bf16[272,1152]{1,0:T(8,128)(2,1)}, u32[]{:S(2)}, u32[]{:S(2)}) collective-permute-start(bf16[272,1152]{1,0:T(8,128)(2,1)S(1)} %concatenate.20.refs_0_), channel_id=1, source_target_pairs={{0,4},{1,5},{2,6},{3,7},{4,0},{5,1},{6,2},{7,3},{8,40},{9,41},{10,... | collective-permute-start | bytes 1880072 | tf_op jit(solution)/shard_map/ppermute | solution.py:34
  36.4 22.1 %collective-permute-start.12 = (bf16[272,1152]{1,0:T(8,128)(2,1)S(1)}, bf16[272,1152]{1,0:T(8,128)(2,1)S(1)}, u32[]{:S(2)}, u32[]{:S(2)}) collective-permute-start(bf16[272,1152]{1,0:T(8,128)(2,1)S(1)} %collective-permute-done.11.refs_2_), channel_id=1, source_target_pairs={{0,8},{1,9},{2,10},{3,11},{4,12},{5,13},{6,14},{7,15},{8,0},{9,1},... | collective-permute-start | bytes 1880072 | tf_op jit(solution)/shard_map/ppermute | solution.py:34
  39.6 30.5 %collective-permute-start.13 = (bf16[272,1152]{1,0:T(8,128)(2,1)}, bf16[272,1152]{1,0:T(8,128)(2,1)}, u32[]{:S(2)}, u32[]{:S(2)}) collective-permute-start(bf16[272,1152]{1,0:T(8,128)(2,1)} %collective-permute-done.10.refs_0_), channel_id=1, source_target_pairs={{0,8},{1,9},{2,10},{3,11},{4,12},{5,13},{6,14},{7,15},{8,0},{9,1},... | collective-permute-start | bytes 1880072 | tf_op jit(solution)/shard_map/ppermute | solution.py:34
  39.7 36.2 %collective-permute-start.8 = (bf16[272,1152]{1,0:T(8,128)(2,1)}, bf16[272,1152]{1,0:T(8,128)(2,1)}, u32[]{:S(2)}, u32[]{:S(2)}) collective-permute-start(bf16[272,1152]{1,0:T(8,128)(2,1)} %collective-permute-done.7.refs_2_), channel_id=1, source_target_pairs={{0,8},{1,9},{2,10},{3,11},{4,12},{5,13},{6,14},{7,15},{8,0},{9,1},... | collective-permute-start | bytes 1880072 | tf_op jit(solution)/shard_map/ppermute | solution.py:34
  49.8 26.1 %collective-permute-start.9 = (bf16[272,1152]{1,0:T(8,128)(2,1)}, bf16[272,1152]{1,0:T(8,128)(2,1)}, u32[]{:S(2)}, u32[]{:S(2)}) collective-permute-start(bf16[272,1152]{1,0:T(8,128)(2,1)} %collective-permute-done.6.refs_0_), channel_id=1, source_target_pairs={{0,8},{1,9},{2,10},{3,11},{4,12},{5,13},{6,14},{7,15},{8,0},{9,1},... | collective-permute-start | bytes 1880072 | tf_op jit(solution)/shard_map/ppermute | solution.py:34
  58.5 23.5 %collective-permute-start.4 = (bf16[272,1152]{1,0:T(8,128)(2,1)}, bf16[272,1152]{1,0:T(8,128)(2,1)S(1)}, u32[]{:S(2)}, u32[]{:S(2)}) collective-permute-start(bf16[272,1152]{1,0:T(8,128)(2,1)} %collective-permute-done.3.refs_2_), channel_id=1, source_target_pairs={{0,8},{1,9},{2,10},{3,11},{4,12},{5,13},{6,14},{7,15},{8,0},{9,1},... | collective-permute-start | bytes 1880072 | tf_op jit(solution)/shard_map/ppermute | solution.py:34
  59.3 22.6 %collective-permute-start.5 = (bf16[272,1152]{1,0:T(8,128)(2,1)}, bf16[272,1152]{1,0:T(8,128)(2,1)S(1)}, u32[]{:S(2)}, u32[]{:S(2)}) collective-permute-start(bf16[272,1152]{1,0:T(8,128)(2,1)} %collective-permute-done.1.refs_0_), channel_id=1, source_target_pairs={{0,8},{1,9},{2,10},{3,11},{4,12},{5,13},{6,14},{7,15},{8,0},{9,1},... | collective-permute-start | bytes 1880072 | tf_op jit(solution)/shard_map/ppermute | solution.py:34
  133.4 11.7 %collective-permute-start.16 = (bf16[288,1152]{1,0:T(8,128)(2,1)}, bf16[288,1152]{1,0:T(8,128)(2,1)S(1)}, u32[]{:S(2)}, u32[]{:S(2)}) collective-permute-start(bf16[288,1152]{1,0:T(8,128)(2,1)} %get-tuple-element.47), channel_id=1, source_target_pairs={{0,2},{1,3},{2,4},{3,5},{4,6},{5,7},{6,0},{7,1},{8,24},{9,25},{10,... | collective-permute-start | bytes 1990664 | tf_op jit(solution)/shard_map/ppermute | solution.py:34
  135.5 9.9 %collective-permute-start.17 = (bf16[288,1152]{1,0:T(8,128)(2,1)}, bf16[288,1152]{1,0:T(8,128)(2,1)S(1)}, u32[]{:S(2)}, u32[]{:S(2)}) collective-permute-start(bf16[288,1152]{1,0:T(8,128)(2,1)} %get-tuple-element.48), channel_id=1, source_target_pairs={{0,6},{1,7},{2,0},{3,1},{4,2},{5,3},{6,4},{7,5},{8,56},{9,57},{10,... | collective-permute-start | bytes 1990664 | tf_op jit(solution)/shard_map/ppermute | solution.py:34
  136.8 16.6 %collective-permute-start.18 = (bf16[288,1152]{1,0:T(8,128)(2,1)}, bf16[288,1152]{1,0:T(8,128)(2,1)S(1)}, u32[]{:S(2)}, u32[]{:S(2)}) collective-permute-start(bf16[288,1152]{1,0:T(8,128)(2,1)} %get-tuple-element.49), channel_id=1, source_target_pairs={{0,4},{1,5},{2,6},{3,7},{4,0},{5,1},{6,2},{7,3},{8,40},{9,41},{10,... | collective-permute-start | bytes 1990664 | tf_op jit(solution)/shard_map/ppermute | solution.py:34
  157.8 8.9 %collective-permute-start.21 = (f32[72,1152]{1,0:T(8,128)S(1)}, f32[72,1152]{1,0:T(8,128)}, u32[]{:S(2)}, u32[]{:S(2)}) collective-permute-start(f32[72,1152]{1,0:T(8,128)S(1)} %get-tuple-element.57), channel_id=1, source_target_pairs={{0,32},{1,33},{2,34},{3,35},{4,36},{5,37},{6,38},{7,39},{8,12},{9,... | collective-permute-start | bytes 995336 | tf_op jit(solution)/shard_map/ppermute | solution.py:34
  170.7 13.5 %collective-permute-start.24 = (f32[72,1152]{1,0:T(8,128)S(1)}, f32[72,1152]{1,0:T(8,128)S(1)}, u32[]{:S(2)}, u32[]{:S(2)}) collective-permute-start(f32[72,1152]{1,0:T(8,128)S(1)} %get-tuple-element.53), channel_id=1, source_target_pairs={{0,1},{1,0},{2,3},{3,2},{4,5},{5,4},{6,7},{7,6},{8,9},{9,8},{10,11... | collective-permute-start | bytes 995336 | tf_op jit(solution)/shard_map/ppermute | solution.py:34
  192.9 11.5 %collective-permute-start.28 = (bf16[288,1152]{1,0:T(8,128)(2,1)S(1)}, bf16[288,1152]{1,0:T(8,128)(2,1)S(1)}, u32[]{:S(2)}, u32[]{:S(2)}) collective-permute-start(bf16[288,1152]{1,0:T(8,128)(2,1)S(1)} %constant_dynamic-update-slice_fusion.refs_0_), channel_id=1, source_target_pairs={{0,2},{1,3},{2,4},{3,5},{4,6},{5,7},{6,0},{7,1},{8,24},{9,25},{10,... | collective-permute-start | bytes 1990664 | tf_op jit(solution)/shard_map/ppermute | solution.py:34
  193.1 17.7 %collective-permute-start.29 = (bf16[288,1152]{1,0:T(8,128)(2,1)S(1)}, bf16[288,1152]{1,0:T(8,128)(2,1)S(1)}, u32[]{:S(2)}, u32[]{:S(2)}) collective-permute-start(bf16[288,1152]{1,0:T(8,128)(2,1)S(1)} %constant_dynamic-update-slice_fusion.refs_0_), channel_id=1, source_target_pairs={{0,6},{1,7},{2,0},{3,1},{4,2},{5,3},{6,4},{7,5},{8,56},{9,57},{10,... | collective-permute-start | bytes 1990664 | tf_op jit(solution)/shard_map/ppermute | solution.py:34
  196.0 16.6 %collective-permute-start.30 = (bf16[288,1152]{1,0:T(8,128)(2,1)S(1)}, bf16[288,1152]{1,0:T(8,128)(2,1)S(1)}, u32[]{:S(2)}, u32[]{:S(2)}) collective-permute-start(bf16[288,1152]{1,0:T(8,128)(2,1)S(1)} %constant_dynamic-update-slice_fusion.refs_0_), channel_id=1, source_target_pairs={{0,4},{1,5},{2,6},{3,7},{4,0},{5,1},{6,2},{7,3},{8,40},{9,41},{10,... | collective-permute-start | bytes 1990664 | tf_op jit(solution)/shard_map/ppermute | solution.py:34
  197.1 21.2 %collective-permute-start.31 = (bf16[288,1152]{1,0:T(8,128)(2,1)S(1)}, bf16[288,1152]{1,0:T(8,128)(2,1)S(1)}, u32[]{:S(2)}, u32[]{:S(2)}) collective-permute-start(bf16[288,1152]{1,0:T(8,128)(2,1)S(1)} %constant_dynamic-update-slice_fusion.refs_0_), channel_id=1, source_target_pairs={{0,8},{1,9},{2,10},{3,11},{4,12},{5,13},{6,14},{7,15},{8,0},{9,1},... | collective-permute-start | bytes 1990664 | tf_op jit(solution)/shard_map/ppermute | solution.py:34
  204.4 13.9 %collective-permute-start.32 = (bf16[288,1152]{1,0:T(8,128)(2,1)S(1)}, bf16[288,1152]{1,0:T(8,128)(2,1)}, u32[]{:S(2)}, u32[]{:S(2)}) collective-permute-start(bf16[288,1152]{1,0:T(8,128)(2,1)S(1)} %collective-permute-done.28.refs_1_), channel_id=1, source_target_pairs={{0,8},{1,9},{2,10},{3,11},{4,12},{5,13},{6,14},{7,15},{8,0},{9,1},... | collective-permute-start | bytes 1990664 | tf_op jit(solution)/shard_map/ppermute | solution.py:34
  (30 other events, 212.2 us)
